TPU v7x, 128 devices: a whole 4x4x4 slice. The times are simulated.
128 devices in a mesh: wide: 16 (over z, y), narrow: 8 (over x, core).
Axes of the slice: x: 4, y: 4, z: 4, core: 2. Of those that a mesh axis runs over, the one named last changes fastest.
Arguments:
- xbc: bfloat16 [65536, 5376], P(('wide', 'narrow')), may hold values from -6 to 6
- conv_weight: float32 [4, 5376], replicated, may hold values from -3 to 3
- conv_bias: float32 [5376], replicated, may hold values from -1 to 0
- dt: float32 [80, 65536], P(None, ('wide', 'narrow')), may hold values from 0 to 1, as said below
- decay_log: float32 [80, 65536], P(None, ('wide', 'narrow')), may hold values from -1 to 0, as said below
- skip: float32 [80], replicated, may hold values from 0.5 to 1.5
Outputs:
- mixed: bfloat16 [65536, 5120], P(('wide', 'narrow'))
Inputs may be any that keep to these rules, and one draw needn't show every extreme that they name: `dt`: step sizes are positive. `decay_log`: entries are at most zero.
All inputs are finite; a program needn't handle non-finite values.
Results may differ from a plain program's by a relative error of at most 0.0053.
Values may be sent and summed in bfloat16 or wider, within the bound.
No kernel may reach another device: no remote copies, remote signals or barrier semaphores. Data moves between devices by JAX's collectives and lax.ppermute only.
A program may use at most 704 MiB of HBM per device.

v0:
```python
import jax
import jax.numpy as jnp
from jax import lax
from jax.sharding import PartitionSpec as P

MIXER_HEADS = 80
HEAD_DIM = 64
N_STATE = 128
CONV = 4
BLOCK = 256
INNER = 5120


def prefix_2(value, axis, join, neutral):
    count, mine = (lax.axis_size(axis), lax.axis_index(axis))
    pieces = jax.tree.map(lambda part: lax.all_gather(part, axis), value)
    running = jax.tree.map(
        lambda part, zero: jnp.full_like(part, 0) + jnp.asarray(zero, part.dtype), value, neutral
    )

    def step(position, running):
        longer = join(running, jax.tree.map(lambda part: part[position], pieces))
        return jax.tree.map(lambda new, old: jnp.where(position < mine, new, old), longer, running)

    return lax.fori_loop(0, count - 1, step, running)


def from_root(shard, axis, root):
    mine = lax.axis_index(axis) == root
    return lax.psum(jnp.where(mine, shard, jnp.zeros_like(shard)), axis)


def shifted(shard, axis, by):
    length = lax.axis_size(axis)
    pairs = [(i, i + by) for i in range(length) if 0 <= i + by < length]
    return lax.ppermute(shard, axis, pairs)


def convolve(kernel_span, conv_weight, conv_bias):
    length = kernel_span.shape[0] - CONV + 1
    running = conv_bias[None, :]
    for offset in range(CONV):
        running = (
            running
            + kernel_span[offset : offset + length].astype(jnp.float32)
            * conv_weight[offset][None, :]
        )
    return jax.nn.silu(running).astype(jnp.bfloat16)


def block_local(element):
    active_flag, step_sizes, log_decays = element
    length = active_flag.shape[0]
    values = active_flag[:, :INNER].reshape(length, MIXER_HEADS, HEAD_DIM)
    inputs = active_flag[:, INNER : INNER + N_STATE]
    readout = active_flag[:, INNER + N_STATE :]
    cumulative = jnp.cumsum(log_decays, axis=1)
    scores = jnp.dot(readout, inputs.T, preferred_element_type=jnp.float32)
    later = lax.broadcasted_iota(jnp.int32, (length, length), 0)
    earlier = lax.broadcasted_iota(jnp.int32, (length, length), 1)
    causal = later >= earlier
    exponent = jnp.minimum(cumulative[:, :, None] - cumulative[:, None, :], 0.0)
    decay = jnp.where(causal[None], jnp.exp(exponent), 0.0)
    weights = (scores[None] * decay * step_sizes[:, None, :]).astype(jnp.bfloat16)
    diagonal_part = jnp.einsum("hts,shp->thp", weights, values, preferred_element_type=jnp.float32)
    to_end = jnp.exp(cumulative[:, -1:] - cumulative) * step_sizes
    loaded = (to_end[:, :, None] * inputs.astype(jnp.float32)[None]).astype(jnp.bfloat16)
    local_state = jnp.einsum("hsn,shp->hpn", loaded, values, preferred_element_type=jnp.float32)
    return (cumulative, diagonal_part, local_state)


def combine_carry(earlier, later):
    return (earlier[0] + later[0], jnp.exp(later[0])[:, None, None] * earlier[1] + later[1])


def within_scan(own_pair, identity):
    prefix = prefix_2(own_pair, "narrow", combine_carry, identity)
    through = combine_carry(prefix, own_pair)
    group_pair = (
        from_root(through[0], "narrow", lax.axis_size("narrow") - 1),
        from_root(through[1], "narrow", lax.axis_size("narrow") - 1),
    )
    return (prefix, group_pair)


def body(xbc, conv_weight, conv_bias, dt, decay_log, skip):
    length_dev = xbc.shape[0]
    blocks_dev = length_dev // BLOCK
    rim_rows = shifted(xbc[length_dev - CONV + 1 :], ("wide", "narrow"), 1)
    active_flag = convolve(jnp.concatenate([rim_rows, xbc], axis=0), conv_weight, conv_bias)
    blocks = active_flag.reshape(blocks_dev, BLOCK, active_flag.shape[1])
    step_all = dt.reshape(MIXER_HEADS, blocks_dev, BLOCK).transpose(1, 0, 2)
    log_all = decay_log.reshape(MIXER_HEADS, blocks_dev, BLOCK).transpose(1, 0, 2)
    cumulative, diagonal_part, local_state = lax.map(block_local, (blocks, step_all, log_all))
    block_logs = cumulative[:, :, -1]

    def advance(state_now, element):
        total_log_decay, piece_state = element
        return (jnp.exp(total_log_decay)[:, None, None] * state_now + piece_state, state_now)

    zero_state = jnp.zeros((MIXER_HEADS, HEAD_DIM, N_STATE), jnp.float32)
    own_state, starts = lax.scan(advance, zero_state, (block_logs, local_state))
    own_log = jnp.sum(block_logs, axis=0)
    prior_logs = jnp.cumsum(block_logs, axis=0) - block_logs
    identity = (jnp.zeros((MIXER_HEADS,), jnp.float32), zero_state)
    own_pair = (own_log, own_state)
    inside_group = within_scan(own_pair, identity)
    prefix, group_pair = inside_group
    before = prefix_2(group_pair, "wide", combine_carry, identity)
    incoming = combine_carry(before, prefix)[1]
    starts = jnp.exp(prior_logs)[:, :, None, None] * incoming[None] + starts
    values = blocks[:, :, :INNER].reshape(blocks_dev, BLOCK, MIXER_HEADS, HEAD_DIM)
    readout = blocks[:, :, INNER + N_STATE :]
    carried = jnp.einsum(
        "ctn,chpn->cthp", readout.astype(jnp.float32), starts, precision=lax.Precision.HIGHEST
    )
    decay_in = jnp.exp(cumulative).transpose(0, 2, 1)[:, :, :, None]
    running = (
        diagonal_part + decay_in * carried + skip[None, None, :, None] * values.astype(jnp.float32)
    )
    return running.reshape(length_dev, INNER).astype(jnp.bfloat16)


def solution(mesh):
    placed = (
        P(("wide", "narrow"), None),
        P(),
        P(),
        P(None, ("wide", "narrow")),
        P(None, ("wide", "narrow")),
        P(),
    )
    return jax.shard_map(
        body, mesh=mesh, in_specs=placed, out_specs=P(("wide", "narrow"), None), check_vma=False
    )
```

profile of v0, /device:TPU:1, one launch (start us, length us, event | category | flops | bytes accessed | tf_op | source)
XLA Modules:
  0.0 695.1 jit_solution(14052222475112877072)
XLA Ops:
  7.5 4.5 collective-permute-start
  15.4 14.2 %multiply_convert_fusion.8 = bf16[512,5376]{1,0:T(8,128)(2,1)} fusion(bf16[512,5376]{1,0:T(8,128)(2,1)} %param.14, bf16[3,5376]{1,0:T(4,128)(2,1)S(1)} %collective-permute-done, f32[5376]{0:T(1024)S(1)} %get-tuple-element.371, f32[5376]{0:T(1024)S(1)} %get-tuple-element.372, f32[5376]{0:T(1024)S(1)} %get-tuple-element.370, f32[5376]{0:T(1024)S(1)} %get-tuple-element.369, ...), kind=kLoop, calls=%fused_computation.45 | loop fusion | flops 71565312 | bytes 11149824 | tf_op jit(solution)/shard_map/convert_element_type | solution.py:48
  29.6 3.0 broadcast.43.clone
  32.6 68.1 %while.57 = (s32[]{:T(128)}, f32[2,80,256]{2,1,0:T(8,128)S(1)}, f32[2,256,80,64]{1,2,3,0:T(8,128)}, f32[2,80,64,128]{3,2,1,0:T(8,128)}, f32[2,80,256]{2,0,1:T(2,...) while((s32[]{:T(128)}, f32[2,80,256]{2,1,0:T(8,128)S(1)}, ...), condition=%wide.region_3.4_spmd, body=%wide.region_0.3_spmd.sunk | while | flops 1062912256 | bytes 127245944 | solution.py:94
  33.8 3.5 constant_dynamic-slice_fusion.8
  37.3 4.6 copy.100
  41.8 1.9 slice.119
  45.2 6.7 fusion.50
  52.0 3.4 copy_dynamic-update-slice_fusion.2
  55.7 3.6 copy-done.5
  60.2 6.2 bitcast_dynamic-update-slice_fusion.4
  67.9 3.5 constant_dynamic-slice_fusion.8
  71.3 4.6 copy.100
  75.9 1.9 slice.119
  79.3 6.7 fusion.50
  86.1 3.4 copy_dynamic-update-slice_fusion.2
  89.8 3.6 copy-done.5
  94.3 6.2 bitcast_dynamic-update-slice_fusion.4
  100.9 3.0 broadcast.43
  104.0 7.7 %while.58 = (s32[]{:T(128)}, f32[80,64,128]{2,1,0:T(8,128)S(1)}, f32[2,80,64,128]{3,2,1,0:T(8,128)}, f32[2,80]{1,0:T(2,128)S(1)}, f32[2,80,64,128]{3,2,1,0:T(8,128)}, /*index=5*/s32[]{:T(128)}, s32[]{:T(128)}) while((s32[]{:T(128)}, f32[80,64,128]{2,1,0:T(8,128)S(1)}, f32[2,80,64,128]{3,2,1,0:T(8,128)}, f32[2,80]{1,0:T(2,128)S(1)}, ...), condition=%wide.region_7.8_spmd.clone, body=%wide.region_6.7_spmd.clone.sunk | while | flops 2621443 | bytes 34080312 | solution.py:102
  104.0 1.9 bitcast_dynamic-update-slice_fusion.5
  105.8 1.6 copy-done.4
  107.8 1.7 bitcast_dynamic-update-slice_fusion.5
  109.5 1.7 copy-done.4
  111.7 1.5 copy-done
  115.0 11.7 %all-reduce = f32[640]{0:T(1024)S(1)} all-reduce(f32[640]{0:T(1024)S(1)} %dynamic-update-slice), channel_id=2, replica_groups=mesh['wide'=16,'narrow'=8] {'narrow'}, use_global_device_ids=true, to_apply=%add | all-reduce | flops 640 | bytes 5120
  126.7 91.2 %all-gather.8.cloned.1.call-done = f32[640,64,128]{2,1,0:T(8,128)} async-done(((f32[80,64,128]{2,1,0:T(8,128)}), f32[640,64,128]{2,1,0:T(8,128)}) %all-gather.8.cloned.1.call-update) | async-done | bytes 20971536 | tf_op jit(solution)/shard_map/all_gather | solution.py:16
  217.9 30.4 %while.59 = (s32[]{:T(128)}, f32[80]{0:T(128)S(1)}, f32[80,64,128]{2,1,0:T(8,128)}, s32[]{:T(128)}, f32[8,80]{1,0:T(8,128)S(1)}, /*index=5*/f32[8,80,64,128]{3,2,1,0:T(8,128)}, s32[]{:T(128)}, s32[]{:T(128)}) while((s32[]{:T(128)}, f32[80]{0:T(128)S(1)}, f32[80,64,128]{2,1,0:T(8,128)}, s32[]{:T(128)}, f32[8,80]{1,0:T(8,128)S(1)}, ...), condition=%wide.region_9.10_spmd.clone, body=%wide.region_8.9_spmd.clone.sunk | while | flops 2621684 | bytes 7866035 | solution.py:25
  217.9 3.8 fusion.52
  221.7 4.4 fusion.52
  226.1 4.4 fusion.52
  230.6 4.4 fusion.52
  235.0 4.4 fusion.52
  239.5 4.4 fusion.52
  243.9 4.4 fusion.52
  248.3 3.6 select_bitcast_fusion
  252.0 66.0 %all-reduce.3.cloned.1.call-done = f32[1,80,64,128]{3,2,1,0:T(8,128)} async-done(((f32[1,80,64,128]{3,2,1,0:T(8,128)}), f32[1,80,64,128]{3,2,1,0:T(8,128)}) %all-reduce.3.cloned.1.call-update) | async-done | bytes 2621456 | tf_op jit(solution)/shard_map/psum | solution.py:30
  318.0 7.8 %slice_convert_fusion.1 = f32[2,256,5120]{2,1,0:T(8,128)} fusion(bf16[2,256,5376]{2,1,0:T(8,128)(2,1)} %get-tuple-element.676), kind=kLoop, calls=%fused_computation.54 | loop fusion | flops 2621440 | bytes 15728640 | tf_op jit(solution)/shard_map/convert_element_type | solution.py:119
  325.8 11.8 %copy.55 = f32[2,256,5120]{1,2,0:T(8,128)} copy(f32[2,256,5120]{2,1,0:T(8,128)} %slice_convert_fusion.1) | data formatting | bytes 20971520 | tf_op jit(solution)/shard_map/convert_element_type | solution.py:119
  337.7 14.7 %psum.14 = f32[1,80]{1,0:T(1,128)S(1)} all-reduce(f32[1,80]{1,0:T(1,128)S(1)} %get-tuple-element.426), channel_id=1, replica_groups=mesh['wide'=16,'narrow'=8] {'narrow'}, use_global_device_ids=true, to_apply=%region_10.11 | all-reduce | flops 80 | bytes 640 | tf_op jit(solution)/shard_map/psum | solution.py:30
  352.4 18.6 %all-gather.2 = f32[16,1,80]{2,1,0:T(1,128)S(1)} all-gather(f32[1,1,80]{2,1,0:T(1,128)S(1)} %bitcast.125), channel_id=1, replica_groups=mesh['wide'=16,'narrow'=8] {'wide'}, dimensions={0}, use_global_device_ids=true | all-gather | bytes 5440 | tf_op jit(solution)/shard_map/all_gather | solution.py:16
  371.1 190.8 %all-gather.6.cloned.1.call-done = f32[16,80,64,128]{3,2,1,0:T(8,128)} async-done(((f32[1,80,64,128]{3,2,1,0:T(8,128)}), f32[16,80,64,128]{3,2,1,0:T(8,128)}) %all-gather.6.cloned.1.call-update) | async-done | bytes 41943056 | tf_op jit(solution)/shard_map/all_gather | solution.py:16
  561.8 66.9 %while.60 = (s32[]{:T(128)}, f32[80,64,128]{2,1,0:T(8,128)}, s32[]{:T(128)}, f32[16,80]{1,0:T(8,128)S(1)}, f32[16,80,64,128]{3,2,1,0:T(8,128)}, /*index=5*/s32[]{:T(128)}, s32[]{:T(128)}) while((s32[]{:T(128)}, f32[80,64,128]{2,1,0:T(8,128)}, s32[]{:T(128)}, f32[16,80]{1,0:T(8,128)S(1)}, f32[16,80,64,128]{3,2,1,0:T(8,128)}, ...), condition=%wide.region_13.14_spmd.clone, body=%wide.region_12.13_spmd.clone.sunk | while | flops 2621444 | bytes 7865385 | solution.py:25
  561.9 3.9 fusion.53
  565.7 4.5 fusion.53
  570.2 4.5 fusion.53
  574.7 4.5 fusion.53
  579.2 4.5 fusion.53
  583.7 4.5 fusion.53
  588.2 4.5 fusion.53
  592.7 4.5 fusion.53
  597.2 4.5 fusion.53
  601.7 4.5 fusion.53
  606.2 4.5 fusion.53
  610.7 4.5 fusion.53
  615.2 4.5 fusion.53
  619.7 4.5 fusion.53
  624.2 4.5 fusion.53
  628.7 2.1 multiply_add_fusion.1
  630.8 3.2 multiply_add_fusion
  634.0 9.4 %fusion.23 = f32[2,256,80,64]{1,2,3,0:T(8,128)S(1)} fusion(f32[2,80,64,128]{3,2,1,0:T(8,128)S(1)} %multiply_add_fusion, bf16[2,256,5376]{2,1,0:T(8,128)(2,1)} %get-tuple-element.676), kind=kOutput, calls=%fused_computation.55 | convolution fusion | flops 4026531840 | bytes 15859712 | tf_op jit(solution)/shard_map/ctn,chpn->cthp/dot_general | solution.py:114
  643.5 13.7 %fusion.20 = bf16[2,256,80,64]{1,2,3,0:T(8,128)(2,1)} fusion(f32[2,256,80,64]{1,3,2,0:T(8,128)S(1)} %bitcast.116, f32[2,256,80,64]{1,2,3,0:T(8,128)} %get-tuple-element.276, f32[2,256,80,64]{1,2,3,0:T(8,128)S(1)} %fusion.23, f32[80]{0:T(128)S(1)} %copy-done.6, f32[2,256,80]{1,2,0:T(8,128)S(1)} %exponential_bitcast_fusion.1), kind=kLoop, calls=%fused_computation.48 | loop fusion | flops 13107200 | bytes 36864320 | tf_op jit(solution)/shard_map/convert_element_type | solution.py:121
  657.1 17.6 %copy.60 = bf16[2,256,80,64]{3,2,1,0:T(8,128)(2,1)} copy(bf16[2,256,80,64]{1,2,3,0:T(8,128)(2,1)} %fusion.20) | data formatting | bytes 10485760 | tf_op jit(solution)/shard_map/convert_element_type | solution.py:121
  674.7 13.9 %reshape.169 = bf16[512,5120]{1,0:T(8,128)(2,1)} reshape(bf16[2,256,80,64]{3,2,1,0:T(8,128)(2,1)} %copy.60) | data formatting | bytes 10485760 | tf_op jit(solution)/shard_map/convert_element_type | solution.py:121
  (127 shorter events, 14.8 us)
Async XLA Ops:
  6.5 211.4 %all-gather.8.cloned.1.call-start = ((), (), s32[]{:S(2)}) async-start(), calls=%async_computation.2 | async-start | bytes 23592960 | tf_op jit(solution)/shard_map/all_gather | solution.py:16
  7.5 7.9 %collective-permute-start = (bf16[3,5376]{1,0:T(4,128)(2,1)S(1)}, bf16[3,5376]{1,0:T(4,128)(2,1)S(1)}, u32[]{:S(2)}, u32[]{:S(2)}) collective-permute-start(bf16[3,5376]{1,0:T(4,128)(2,1)S(1)} %slice.53), channel_id=1, source_target_pairs={{0,1},{1,2},{2,3},{3,4},{4,5},{5,6},{6,7},{7,8},{8,9},{9,10},{10,1... | collective-permute-start | bytes 96776 | tf_op jit(solution)/shard_map/ppermute | solution.py:36
  43.8 8.2 %copy-start.3 = (bf16[256,5120]{0,1:T(8,128)(2,1)}, bf16[256,5120]{0,1:T(8,128)(2,1)S(1)}, u32[]{:S(2)}) copy-start(bf16[256,5120]{0,1:T(8,128)(2,1)S(1)} %slice.119) | copy-start | bytes 7864324 | tf_op jit(solution)/shard_map/while
  43.8 8.2 %slice-start.3 = ((s8[10485760]{0:T(1024)(128)(4,1)}), s8[4194304]{0:T(1024)(128)(4,1)S(1)}, s32[]{:S(2)}) async-start(s8[10485760]{0:T(1024)(128)(4,1)} %bitcast.117), calls=%async_computation.6 | async-start | bytes 8388608 | tf_op jit(solution)/shard_map/while
  45.2 6.7 slice-start.4
  45.2 6.7 slice-start.5
  55.4 3.9 copy-start.5
  77.8 8.2 %copy-start.3 = (bf16[256,5120]{0,1:T(8,128)(2,1)}, bf16[256,5120]{0,1:T(8,128)(2,1)S(1)}, u32[]{:S(2)}) copy-start(bf16[256,5120]{0,1:T(8,128)(2,1)S(1)} %slice.119) | copy-start | bytes 7864324 | tf_op jit(solution)/shard_map/while
  77.8 8.2 %slice-start.3 = ((s8[10485760]{0:T(1024)(128)(4,1)}), s8[4194304]{0:T(1024)(128)(4,1)S(1)}, s32[]{:S(2)}) async-start(s8[10485760]{0:T(1024)(128)(4,1)} %bitcast.117), calls=%async_computation.6 | async-start | bytes 8388608 | tf_op jit(solution)/shard_map/while
  79.3 6.7 slice-start.4
  79.3 6.7 slice-start.5
  89.4 3.9 copy-start.5
  104.0 9.3 %copy-start.7 = (u32[128]{0:T(128)S(1)}, u32[128]{0:T(128)}, u32[]{:S(2)}) copy-start(u32[128]{0:T(128)} %constant.104) | copy-start | bytes 1540
  104.0 3.4 copy-start.4
  107.8 3.4 copy-start.4
  111.7 1.5 copy-start
  113.2 204.8 %all-reduce.3.cloned.1.call-start = ((), (), s32[]{:S(2)}) async-start(), calls=%async_computation | async-start | bytes 5242880 | tf_op jit(solution)/shard_map/psum | solution.py:30
  217.9 30.4 %copy-start.1 = (f32[80,64,128]{2,1,0:T(8,128)S(1)}, f32[80,64,128]{2,1,0:T(8,128)}, u32[]{:S(2)}) copy-start(f32[80,64,128]{2,1,0:T(8,128)} %copy-done) | copy-start | bytes 7864324
  252.0 309.9 %all-gather.6.cloned.1.call-start = ((), (), s32[]{:S(2)}) async-start(), calls=%async_computation.1 | async-start | bytes 44564480 | tf_op jit(solution)/shard_map/all_gather | solution.py:16
  561.8 66.9 %copy-start.2 = (f32[80,64,128]{2,1,0:T(8,128)S(1)}, f32[80,64,128]{2,1,0:T(8,128)}, u32[]{:S(2)}) copy-start(f32[80,64,128]{2,1,0:T(8,128)} %get-tuple-element.281) | copy-start | bytes 7864324
  630.8 12.6 %slice-start = ((s8[10485760]{0:T(1024)(128)(4,1)}), s8[4194304]{0:T(1024)(128)(4,1)S(1)}, s32[]{:S(2)}) async-start(s8[10485760]{0:T(1024)(128)(4,1)} %bitcast.114), calls=%async_computation.3 | async-start | bytes 8388608
  634.0 9.4 %slice-start.1 = ((s8[10485760]{0:T(1024)(128)(4,1)}), s8[4194304]{0:T(1024)(128)(4,1)S(1)}, s32[]{:S(2)}) async-start(s8[10485760]{0:T(1024)(128)(4,1)} %bitcast.114), calls=%async_computation.4 | async-start | bytes 8388608
  634.0 9.4 %slice-start.2 = ((s8[10485760]{0:T(1024)(128)(4,1)}), s8[2097152]{0:T(1024)(128)(4,1)S(1)}, s32[]{:S(2)}) async-start(s8[10485760]{0:T(1024)(128)(4,1)} %bitcast.114), calls=%async_computation.5 | async-start | bytes 4194304
  634.0 9.4 %copy-start.6 = (f32[80]{0:T(128)S(1)}, f32[80]{0:T(128)}, u32[]{:S(2)}) copy-start(f32[80]{0:T(128)} %param.19) | copy-start | bytes 964
Sparse Core Ops, SparseCore 0:
  113.3 104.5 all-gather.7
  252.1 65.8 all-reduce.2
  320.1 241.6 all-gather.5
where the time goes:
time: 697 us; the launch traced here: 695 us
  waiting for transfers between devices  348 us (50%)
  other arithmetic  150 us (22%)
  local copies, waits for them, and re-layouts  95.2 us (14%)
  blocking collectives  45 us (6%)
  matrix products  38 us (5%)
  between operations  14 us (2%)
    all_gather x2, waiting for transfers between devices, prefix_2(): pieces = jax.tree.map(lambda part: lax.all_gather(part, axis), value)  282 us
    select_n x22, other arithmetic, step(): jnp.where(position < mine, new, old)  97 us
    psum x1, waiting for transfers between devices, from_root(): return lax.psum(jnp.where(mine, shard, jnp.zeros_like(shard)), axis)  66 us
    convert_element_type x2, local copies, waits for them, and re-layouts, body(): return running.reshape(length_dev, INNER).astype(jnp.bfloat16)  31.5 us
    all_gather x1, blocking collectives, prefix_2(): pieces = jax.tree.map(lambda part: lax.all_gather(part, axis), value)  18.6 us
    dynamic_slice x8, local copies, waits for them, and re-layouts, body(): lax.map(block_local, (blocks, step_all, log_all))  16.5 us
    psum x1, blocking collectives, from_root(): return lax.psum(jnp.where(mine, shard, jnp.zeros_like(shard)), axis)  14.7 us
    convert_element_type x1, other arithmetic, convolve(): return jax.nn.silu(running).astype(jnp.bfloat16)  14.2 us
  transfers between devices with their start and end apart: 4, of which 3 were waited for; matrix products, arithmetic and copies ran while one was open for 3% of the time, Pallas kernels for 0%

commit v1 on v0

v1 whole, which is shorter than its diff:
```python
import jax
import jax.numpy as jnp
from jax import lax
from jax.experimental import pallas as pl
from jax.experimental.pallas import tpu as pltpu
from jax.sharding import PartitionSpec as P

HEADS = 80
HEAD_DIM = 64
N_STATE = 128
CONV = 4
INNER = 5120
TOK = 512
CHUNK = 128
CHUNKS = TOK // CHUNK
TILE = 512
TILES = INNER // TILE
GROUPS = TILE // 128
ROWS = INNER // 128
SENT = 48
LANES = 128
ALL = ("wide", "narrow")
F32 = jnp.float32
BF16 = jnp.bfloat16


def dot(a, b):
    return jnp.dot(a, b, preferred_element_type=F32)


def dot_nt(a, b, precision=None):
    return lax.dot_general(
        a, b, (((1,), (1,)), ((), ())), preferred_element_type=F32, precision=precision
    )


def iota(shape, dim):
    return lax.broadcasted_iota(jnp.int32, shape, dim)


def split_pair(value):
    high = value.astype(BF16)
    low = (value - high.astype(F32)).astype(BF16)
    return jnp.concatenate([high, low], axis=1)


def pad_heads(value):
    return jnp.concatenate(
        [value, jnp.zeros((value.shape[0], LANES - HEADS), value.dtype)], axis=1
    )


def spread(tile):
    head = iota((2 * LANES, TILE), 0) % LANES
    lane = iota((2 * LANES, TILE), 1) // HEAD_DIM
    return (head == lane + tile * (TILE // HEAD_DIM)).astype(F32).astype(BF16)


def conv_tile(x_ref, rim_ref, weight_ref, bias_ref, span_ref, width):
    span_ref[0:8, 0:width] = rim_ref[...].astype(F32)
    span_ref[8 : 8 + TOK, 0:width] = x_ref[...].astype(F32)
    running = bias_ref[...]
    for k in range(CONV):
        running = running + span_ref[5 + k : 5 + k + TOK, 0:width] * weight_ref[k : k + 1, :]
    half = 0.5 * running
    return (half + half * jnp.tanh(half)).astype(BF16)


def chunk_decays(dt_ref, log_ref, chunk):
    rows, cols = iota((CHUNK, CHUNK), 0), iota((CHUNK, CHUNK), 1)
    lower = (rows >= cols).astype(F32)
    unit = (rows == cols).astype(F32)
    span = slice(chunk * CHUNK, (chunk + 1) * CHUNK)
    cumulative = dot_nt(lower, log_ref[:, span], lax.Precision.HIGHEST)
    steps = dot_nt(unit, dt_ref[:, span], lax.Precision.HIGHEST)
    whole = cumulative[CHUNK - 1 :, :]
    middle = 0.5 * whole
    to_middle = jnp.exp(middle - cumulative) * steps
    from_middle = jnp.exp(cumulative - middle)
    return to_middle, from_middle, whole


def state_kernel(
    x_ref, side_ref, rim_ref, rim_side_ref, weight_ref, weight_side_ref, bias_ref, bias_side_ref,
    dt_ref, log_ref,
    values_ref, side_out_ref, sent_ref, factors_ref, halves_ref,
    span_ref, inputs_ref, held_ref,
):
    tile = pl.program_id(0)

    @pl.when(tile == 0)
    def _():
        side = conv_tile(
            side_ref, rim_side_ref, weight_side_ref, bias_side_ref, span_ref, 2 * N_STATE
        )
        side_out_ref[...] = side
        inputs_ref[...] = side[:, 0:N_STATE].astype(F32).T.astype(BF16)
        totals = []
        for q in range(CHUNKS):
            to_middle, from_middle, whole = chunk_decays(dt_ref, log_ref, q)
            span = slice(q * CHUNK, (q + 1) * CHUNK)
            factors_ref[span, 0 : 2 * LANES] = split_pair(pad_heads(to_middle))
            factors_ref[span, 2 * LANES :] = split_pair(pad_heads(from_middle))
            totals.append(whole)
        all_four = jnp.concatenate(totals + [jnp.zeros((8 - CHUNKS, HEADS), F32)], axis=0)
        halves_ref[...] = split_pair(pad_heads(jnp.exp(0.5 * all_four)))
        decay = pad_heads(jnp.exp(totals[0] + totals[1] + totals[2] + totals[3]))
        high = decay.astype(BF16).astype(F32)
        middle = (decay - high).astype(BF16).astype(F32)
        low = decay - high - middle
        tail = jnp.concatenate([high, middle, low, jnp.zeros((5, LANES), F32)], axis=0)
        sent_ref[:, ROWS:, :] = jnp.broadcast_to(tail[None], (N_STATE, 8, LANES)).astype(BF16)

    values = conv_tile(x_ref, rim_ref, weight_ref, bias_ref, span_ref, TILE)
    values_ref[...] = values
    wide = spread(tile)
    halves = dot(halves_ref[...], wide)
    state = jnp.zeros((N_STATE, TILE), F32)
    for q in range(CHUNKS):
        span = slice(q * CHUNK, (q + 1) * CHUNK)
        scale = dot(factors_ref[span, 0 : 2 * LANES], wide)
        scaled = (values[span].astype(F32) * scale).astype(BF16)
        local = dot(inputs_ref[:, span], scaled)
        half = halves[q : q + 1, :]
        state = half * (half * state + local)
    for g in range(GROUPS):
        held_ref[pl.ds(tile * GROUPS + g, N_STATE, stride=ROWS), :] = state[
            :, g * LANES : (g + 1) * LANES
        ]

    @pl.when(tile == TILES - 1)
    def _():
        def move(n, _):
            sent_ref[n, 0:ROWS, :] = held_ref[
                pl.ds(pl.multiple_of(n * ROWS, 8), ROWS), :
            ].astype(BF16)
            return 0

        lax.fori_loop(0, N_STATE, move, 0)


def scan_kernel(count, pieces_ref, out_ref, decay_ref):
    tails = pieces_ref[:, ROWS:, :].astype(F32)
    decay = jnp.sum(tails, axis=1)
    factors = split_pair(decay)
    for t in range(TILES):
        wide = dot(factors, spread(t))
        for g in range(GROUPS):
            decay_ref[pl.ds(t * GROUPS + g, count, stride=ROWS), :] = wide[
                :, g * LANES : (g + 1) * LANES
            ]

    def step(i, running):
        out_ref[i] = running.astype(BF16)
        piece = pieces_ref[i, 0:ROWS, :].astype(F32)
        return decay_ref[pl.ds(pl.multiple_of(i * ROWS, 8), ROWS), :] * running + piece

    lax.fori_loop(0, count, step, jnp.zeros((ROWS, LANES), F32))


def mix_kernel(
    values_ref, side_ref, factors_ref, halves_ref, start_ref, skip_ref,
    out_ref, both_ref, inputs_ref, held_ref,
):
    tile = pl.program_id(0)

    @pl.when(tile == 0)
    def _():
        side = side_ref[...]
        inputs_ref[...] = side[:, 0:N_STATE].astype(F32).T.astype(BF16)
        rows, cols = iota((CHUNK, CHUNK), 0), iota((CHUNK, CHUNK), 1)
        for q in range(CHUNKS):
            span = slice(q * CHUNK, (q + 1) * CHUNK)
            readout = side[span, N_STATE:]
            scores = dot_nt(readout, side[span, 0:N_STATE])
            both_ref[span, 0:CHUNK] = jnp.where(rows >= cols, scores, 0.0).astype(BF16)
            both_ref[span, CHUNK:] = readout

        def move(n, _):
            held_ref[pl.ds(pl.multiple_of(n * ROWS, 8), ROWS), :] = start_ref[n].astype(F32)
            return 0

        lax.fori_loop(0, N_STATE, move, 0)

    wide = spread(tile)
    halves = dot(halves_ref[...], wide)
    state = jnp.concatenate(
        [
            held_ref[pl.ds(tile * GROUPS + g, N_STATE, stride=ROWS), :]
            for g in range(GROUPS)
        ],
        axis=1,
    )
    for q in range(CHUNKS):
        span = slice(q * CHUNK, (q + 1) * CHUNK)
        values = values_ref[span, :].astype(F32)
        scaled = (values * dot(factors_ref[span, 0 : 2 * LANES], wide)).astype(BF16)
        half = halves[q : q + 1, :]
        begin = half * state
        mixed = dot(both_ref[span, :], jnp.concatenate([scaled, begin.astype(BF16)], axis=0))
        rise = dot(factors_ref[span, 2 * LANES :], wide)
        out_ref[span, :] = (mixed * rise + skip_ref[...] * values).astype(BF16)
        if q < CHUNKS - 1:
            state = half * (begin + dot(inputs_ref[:, span], scaled))


def whole(shape):
    return pl.BlockSpec(shape, lambda j: (0,) * len(shape))


def body(xbc, conv_weight, conv_bias, dt, decay_log, skip):
    count = lax.axis_size(ALL)
    rim = lax.ppermute(xbc[TOK - 8 :], ALL, [(i, i + 1) for i in range(count - 1)])
    bias = conv_bias[None, :]
    column = lambda rows: pl.BlockSpec((rows, TILE), lambda j: (0, j))
    side = lambda rows: pl.BlockSpec((rows, 2 * N_STATE), lambda j: (0, INNER // (2 * N_STATE)))
    big = pltpu.CompilerParams(
        dimension_semantics=("arbitrary",), vmem_limit_bytes=48 * 1024 * 1024
    )
    values, sides, sent, factors, halves = pl.pallas_call(
        state_kernel,
        grid=(TILES,),
        in_specs=[
            column(TOK), side(TOK), column(8), side(8), column(CONV), side(CONV), column(1), side(1),
            whole((HEADS, TOK)), whole((HEADS, TOK)),
        ],
        out_specs=[
            column(TOK), whole((TOK, 2 * N_STATE)), whole((N_STATE, SENT, LANES)),
            whole((TOK, 4 * LANES)), whole((8, 2 * LANES)),
        ],
        out_shape=[
            jax.ShapeDtypeStruct((TOK, INNER), BF16),
            jax.ShapeDtypeStruct((TOK, 2 * N_STATE), BF16),
            jax.ShapeDtypeStruct((N_STATE, SENT, LANES), BF16),
            jax.ShapeDtypeStruct((TOK, 4 * LANES), BF16),
            jax.ShapeDtypeStruct((8, 2 * LANES), BF16),
        ],
        scratch_shapes=[
            pltpu.VMEM((8 + TOK, TILE), F32),
            pltpu.VMEM((N_STATE, TOK), BF16),
            pltpu.VMEM((N_STATE * ROWS, LANES), F32),
        ],
        compiler_params=big,
        name="local_states",
    )(xbc, xbc, rim, rim, conv_weight, conv_weight, bias, bias, dt, decay_log)
    pieces = lax.all_to_all(sent, ALL, 0, 0, tiled=True)
    prefixes = pl.pallas_call(
        lambda *refs: scan_kernel(count, *refs),
        out_shape=jax.ShapeDtypeStruct((count, ROWS, LANES), BF16),
        scratch_shapes=[pltpu.VMEM((count * ROWS, LANES), F32)],
        compiler_params=pltpu.CompilerParams(vmem_limit_bytes=48 * 1024 * 1024),
        name="scan_devices",
    )(pieces)
    starts = lax.all_to_all(prefixes, ALL, 0, 0, tiled=True)
    skips = jnp.repeat(skip, HEAD_DIM)[None, :]
    return pl.pallas_call(
        mix_kernel,
        grid=(TILES,),
        in_specs=[
            column(TOK), whole((TOK, 2 * N_STATE)), whole((TOK, 4 * LANES)),
            whole((8, 2 * LANES)), whole((N_STATE, ROWS, LANES)), column(1),
        ],
        out_specs=column(TOK),
        out_shape=jax.ShapeDtypeStruct((TOK, INNER), BF16),
        scratch_shapes=[
            pltpu.VMEM((TOK, 2 * LANES), BF16),
            pltpu.VMEM((N_STATE, TOK), BF16),
            pltpu.VMEM((N_STATE * ROWS, LANES), F32),
        ],
        compiler_params=big,
        name="mix",
    )(values, sides, factors, halves, starts, skips)


def solution(mesh):
    placed = (P(ALL, None), P(), P(), P(None, ALL), P(None, ALL), P())
    return jax.shard_map(
        body, mesh=mesh, in_specs=placed, out_specs=P(ALL, None), check_vma=False
    )
```

time: 697 us -> 116 us (0.17)
  waiting for transfers between devices: 348 us -> 22.9 us
  other arithmetic: 150 us -> 0 us
  local copies, waits for them, and re-layouts: 95.2 us -> 4.54 us
  Pallas kernels: 0 us -> 43 us
  matrix products: 38 us -> 0 us
  between operations: 14 us -> 0.04 us
  blocking collectives: 45 us -> 36 us
    all_gather x2 -> x0, waiting for transfers between devices: 282 us -> none  [prefix_2(): pieces = jax.tree.map(lambda part: lax.all_gather(part, axis), value)]
    select_n x22 -> x0, other arithmetic: 97 us -> none  [step(): jnp.where(position < mine, new, old)]
    psum x1 -> x0, waiting for transfers between devices: 66 us -> none  [from_root(): return lax.psum(jnp.where(mine, shard, jnp.zeros_like(shard)), axis)]
    convert_element_type x5 -> x0, local copies, waits for them, and re-layouts: 43.5 us -> none  [the longest x2 31.5 us: body(): return running.reshape(length_dev, INNER).astype(jnp.bfloat16)]
    pallas_call x0 -> x3, Pallas kernels: none -> 43 us  [the longest x1 23.5 us: body(): pl.pallas_call(state_kernel, grid=(TILES,), in_specs=[column(TOK), side(T...]
    dot_general x7 -> x0, matrix products: 38 us -> none  [the longest x2 13.4 us: block_local(): jnp.einsum('hts,shp->thp', weights, values, preferred_element_type=jnp.fl...]
    convert_element_type x5 -> x0, other arithmetic: 37.4 us -> none  [the longest x1 14.2 us: convolve(): return jax.nn.silu(running).astype(jnp.bfloat16)]
    all_to_all x0 -> x1, blocking collectives: none -> 36 us  [body(): pieces = lax.all_to_all(sent, ALL, 0, 0, tiled=True)]
  transfers between devices with their start and end apart: 4 -> 2, of which waited for: 3 -> 2; matrix products, arithmetic and copies ran while one was open for 3% -> 1% of each run, Pallas kernels for 0% -> 0%
where the time goes in v1:
time: 116 us; the launch traced here: 115 us
  Pallas kernels  43 us (37%)
  blocking collectives  36 us (31%)
  waiting for transfers between devices  22.9 us (20%)
  starting transfers between devices  8.97 us (8%)
  local copies, waits for them, and re-layouts  4.54 us (4%)
    all_to_all x1, blocking collectives, body(): pieces = lax.all_to_all(sent, ALL, 0, 0, tiled=True)  36 us
    pallas_call x1, Pallas kernels, body(): pl.pallas_call(state_kernel, grid=(TILES,), in_specs=[column(TOK), side(T...  23.5 us
    all_to_all x1, waiting for transfers between devices, body(): starts = lax.all_to_all(prefixes, ALL, 0, 0, tiled=True)  22.1 us
    pallas_call x1, Pallas kernels, body(): pl.pallas_call(mix_kernel, grid=(TILES,), in_specs=[column(TOK), whole((T...  16.6 us
    ppermute x1, starting transfers between devices, body(): lax.ppermute(xbc[TOK - 8:], ALL, [(i, i + 1) for i in range(count - 1)])  4.5 us
    all_to_all x1, starting transfers between devices, body(): starts = lax.all_to_all(prefixes, ALL, 0, 0, tiled=True)  4.47 us
    pallas_call x1, Pallas kernels, body(): pl.pallas_call(lambda *refs: scan_kernel(count, *refs), out_shape=jax.Sha...  2.9 us
    unnamed x8, local copies, waits for them, and re-layouts  2.72 us
  transfers between devices with their start and end apart: 2, of which 2 were waited for; matrix products, arithmetic and copies ran while one was open for 1% of the time, Pallas kernels for 0%

profile of v1, /device:TPU:1, one launch (start us, length us, event | category | flops | bytes accessed | tf_op | source)
XLA Modules:
  0.0 115.4 jit_solution(4836936194621008601)
XLA Ops:
  0.0 0.9 slice.3
  0.9 4.5 %collective-permute-start = (bf16[8,5376]{1,0:T(8,128)(2,1)S(1)}, bf16[8,5376]{1,0:T(8,128)(2,1)S(1)}, u32[]{:S(2)}, u32[]{:S(2)}) collective-permute-start(bf16[8,5376]{1,0:T(8,128)(2,1)S(1)} %slice.3), channel_id=1, source_target_pairs={{0,1},{1,2},{2,3},{3,4},{4,5},{5,6},{6,7},{7,8},{8,9},{9,10},{10,1... | collective-permute-start | bytes 258056 | tf_op jit(solution)/shard_map/ppermute | solution.py:213
  5.4 0.8 broadcast_in_dim.6.bias_ref.bias_side_ref
  6.2 0.7 collective-permute-done.rim_ref.rim_side_ref
  6.9 0.0 copy-start
  6.9 0.9 copy-done
  7.8 0.0 copy-start.1
  7.8 0.9 copy-done.1
  8.7 0.0 copy-start.2
  8.7 0.9 copy-done.2
  9.6 23.5 %local_states.1 = (bf16[512,5120]{1,0:T(8,128)(2,1)}, bf16[512,256]{1,0:T(8,128)(2,1)S(1)}, bf16[128,48,128]{2,1,0:T(8,128)(2,1)S(1)}, bf16[512,512]{1,0:T(8,128)(2,1)S(1)}, bf16[8,256]{1,0:T(8,128)(2,1)S(1)}) custom-call(bf16[512,5376]{1,0:T(8,128)(2,1)} %side_ref.1, bf16[512,5376]{1,0:T(8,128)(2,1)} %side_ref.1, ...), custom_call_target="tpu_custom_call" | custom-call | tf_op jit(solution)/shard_map/local_states/pallas_call | solution.py:220
  33.2 36.0 %all_to_all.10.refs_0_ = bf16[128,48,128]{2,1,0:T(8,128)(2,1)S(1)} all-to-all(bf16[128,48,128]{2,1,0:T(8,128)(2,1)S(1)} %get-tuple-element.14), channel_id=1, replica_groups=mesh['wide'=16,'narrow'=8] {'wide','narrow'}, dimensions={0} | all-to-all | bytes 3145728 | tf_op jit(solution)/shard_map/all_to_all | solution.py:246
  69.2 2.9 %scan_devices.1 = bf16[128,40,128]{2,1,0:T(8,128)(2,1)} custom-call(bf16[128,48,128]{2,1,0:T(8,128)(2,1)S(1)} %all_to_all.10.refs_0_), custom_call_target="tpu_custom_call" | custom-call | tf_op jit(solution)/shard_map/scan_devices/pallas_call | solution.py:247
  72.1 0.0 copy-start.3
  72.1 4.5 %all-to-all-start.1 = ((bf16[128,40,128]{2,1,0:T(8,128)(2,1)}), bf16[128,40,128]{2,1,0:T(8,128)(2,1)S(1)}, u32[]{:S(2)}, u32[]{:S(2)}) async-start(bf16[128,40,128]{2,1,0:T(8,128)(2,1)} %scan_devices.1), calls=%async_computation.1 | async-start | bytes 2621440 | tf_op jit(solution)/shard_map/all_to_all | solution.py:254
  76.5 0.0 copy-done.3
  76.5 0.1 broadcast_in_dim.7
  76.6 0.1 broadcast_in_dim_reshape.3.skip_ref
  76.7 22.1 %all-to-all-done.1.start_ref = bf16[128,40,128]{2,1,0:T(8,128)(2,1)S(1)} async-done(((bf16[128,40,128]{2,1,0:T(8,128)(2,1)}), bf16[128,40,128]{2,1,0:T(8,128)(2,1)S(1)}, u32[]{:S(2)}, u32[]{:S(2)}) %all-to-all-start.1) | async-done | bytes 1310752 | tf_op jit(solution)/shard_map/all_to_all | solution.py:254
  98.8 16.6 %mix.1 = bf16[512,5120]{1,0:T(8,128)(2,1)} custom-call(bf16[512,5120]{1,0:T(8,128)(2,1)} %get-tuple-element.10.values_ref, bf16[512,256]{1,0:T(8,128)(2,1)S(1)} %get-tuple-element.11.side_ref, bf16[512,512]{1,0:T(8,128)(2,1)S(1)} %get-tuple-element.12.factors_ref, bf16[8,256]{1,0:T(8,128)(2,1)S(1)} %get-tuple-element.13.halves_ref, ...), custom_call_target="tpu_custom_call" | custom-call | tf_op jit(solution)/shard_map/mix/pallas_call | solution.py:256
Async XLA Ops:
  0.9 6.0 %collective-permute-start = (bf16[8,5376]{1,0:T(8,128)(2,1)S(1)}, bf16[8,5376]{1,0:T(8,128)(2,1)S(1)}, u32[]{:S(2)}, u32[]{:S(2)}) collective-permute-start(bf16[8,5376]{1,0:T(8,128)(2,1)S(1)} %slice.3), channel_id=1, source_target_pairs={{0,1},{1,2},{2,3},{3,4},{4,5},{5,6},{6,7},{7,8},{8,9},{9,10},{10,1... | collective-permute-start | bytes 258056 | tf_op jit(solution)/shard_map/ppermute | solution.py:213
  6.9 0.9 copy-start
  7.8 0.9 copy-start.1
  8.7 0.9 copy-start.2
  72.1 4.5 %copy-start.3 = (f32[80]{0:T(128)S(1)}, f32[80]{0:T(128)}, u32[]{:S(2)}) copy-start(f32[80]{0:T(128)} %param.11) | copy-start | bytes 964
  72.1 26.8 %all-to-all-start.1 = ((bf16[128,40,128]{2,1,0:T(8,128)(2,1)}), bf16[128,40,128]{2,1,0:T(8,128)(2,1)S(1)}, u32[]{:S(2)}, u32[]{:S(2)}) async-start(bf16[128,40,128]{2,1,0:T(8,128)(2,1)} %scan_devices.1), calls=%async_computation.1 | async-start | bytes 2621440 | tf_op jit(solution)/shard_map/all_to_all | solution.py:254

commit v2 on v0

v2 whole, which is shorter than its diff:
```python
import jax
import jax.numpy as jnp
from jax import lax
from jax.experimental import pallas as pl
from jax.experimental.pallas import tpu as pltpu
from jax.sharding import PartitionSpec as P

HEADS = 80
HEAD_DIM = 64
N_STATE = 128
CONV = 4
INNER = 5120
WIDTH = INNER + 2 * N_STATE
TOK = 512
CHUNK = 128
CHUNKS = TOK // CHUNK
LANES = 128
TILE = 512
TILES = INNER // TILE
GROUPS = TILE // LANES
PIECE = 64
HALF_TILES = TILES // 2
HALF_GROUPS = INNER // LANES // 2
PAIRS = N_STATE // 2
ROWS = 2 * HALF_GROUPS
SENT = ROWS + 8
ALL = ("wide", "narrow")
F32 = jnp.float32
BF16 = jnp.bfloat16
MIB = 1024 * 1024


def dot(a, b):
    return jnp.dot(a, b, preferred_element_type=F32)


def dot_nt(a, b, precision=None):
    return lax.dot_general(
        a, b, (((1,), (1,)), ((), ())), preferred_element_type=F32, precision=precision
    )


def iota(shape, dim):
    return lax.broadcasted_iota(jnp.int32, shape, dim)


def split_pair(value):
    high = value.astype(BF16)
    low = (value - high.astype(F32)).astype(BF16)
    return jnp.concatenate([high, low], axis=1)


def pad_heads(value):
    return jnp.concatenate(
        [value, jnp.zeros((value.shape[0], LANES - HEADS), value.dtype)], axis=1
    )


def spread(tile):
    head = iota((2 * LANES, TILE), 0) % LANES
    lane = iota((2 * LANES, TILE), 1) // HEAD_DIM
    return (head == lane + tile * (TILE // HEAD_DIM)).astype(F32).astype(BF16)


def core_index():
    return lax.rem(lax.axis_index("narrow"), 2)


def running_decay(log_ref, dt_ref, chunk):
    rows, cols = iota((CHUNK, CHUNK), 0), iota((CHUNK, CHUNK), 1)
    lower = (rows >= cols).astype(F32)
    unit = (rows == cols).astype(F32)
    span = slice(chunk * CHUNK, (chunk + 1) * CHUNK)
    cumulative = dot_nt(lower, log_ref[:, span], lax.Precision.HIGHEST)
    steps = dot_nt(unit, dt_ref[:, span], lax.Precision.HIGHEST)
    return cumulative, steps


def thirds(row):
    high = row.astype(BF16).astype(F32)
    middle = (row - high).astype(BF16).astype(F32)
    low = row - high - middle
    return jnp.concatenate([high, middle, low, jnp.zeros((5, LANES), F32)], axis=0)


def fetch_kernel(x_hbm, dt_ref, log_ref, x_ref, to_end_ref, tail_ref, sem):
    copy = pltpu.make_async_copy(x_hbm, x_ref, sem)
    copy.start()
    after = jnp.zeros((1, HEADS), F32)
    for q in reversed(range(CHUNKS)):
        cumulative, steps = running_decay(log_ref, dt_ref, q)
        total = cumulative[CHUNK - 1 :, :]
        to_end = jnp.exp(total - cumulative + after) * steps
        to_end_ref[q * CHUNK : (q + 1) * CHUNK, :] = split_pair(pad_heads(to_end))
        after = after + total
    tail_ref[...] = thirds(pad_heads(jnp.exp(after)))
    copy.wait()


def conv_lanes(x_ref, rim_ref, weight_ref, bias_ref, span_ref, lane, after):
    lanes = pl.ds(lane, LANES)
    span_ref[0:8, :] = rim_ref[:, lanes].astype(F32)
    for row in range(0, TOK, PIECE):
        span_ref[8 + row : 8 + row + PIECE, :] = x_ref[row : row + PIECE, lanes].astype(F32)
    taps = [0.5 * weight_ref[k : k + 1, lanes] for k in range(CONV)]
    start = 0.5 * bias_ref[:, lanes]
    for row in range(0, TOK, PIECE):
        half = start
        for k in range(CONV):
            half = half + span_ref[5 + k + row : 5 + k + row + PIECE, :] * taps[k]
        after((half + half * jnp.tanh(half)).astype(BF16), row)


def tile_lanes(t):
    return pl.ds(pl.multiple_of(t * TILE, TILE), TILE)


def half_of(own):
    return core_index() if own else 1 - core_index()


def side_values(x_ref, rim_ref, weight_ref, bias_ref, span_ref, side_ref, inputs_ref):
    for g in range(2):

        def keep(values, row, g=g):
            side_ref[row : row + PIECE, g * LANES : (g + 1) * LANES] = values

        conv_lanes(
            x_ref, rim_ref, weight_ref, bias_ref, span_ref.at[g], INNER + g * LANES, keep
        )
    inputs_ref[...] = side_ref[:, 0:N_STATE].astype(F32).T.astype(BF16)


def state_kernel(
    own, x_ref, rim_ref, weight_ref, bias_ref, to_end_ref, tail_ref, inputs_ref,
    values_hbm, state_ref, *rest,
):
    span_ref, held_ref, scale_ref, loaded_ref, values_ref, sems = rest[-6:]
    spare_hbm = rest[0]
    half = half_of(own)

    def values_copy(t):
        return pltpu.make_async_copy(
            values_ref.at[t], values_hbm.at[:, tile_lanes(t)], sems.at[t]
        )

    def load(t, slot):
        scale_ref[slot] = dot(to_end_ref[...], spread(half * HALF_TILES + t))
        for g in range(GROUPS):
            lane = pl.multiple_of(half * (INNER // 2) + t * TILE + g * LANES, LANES)
            local = slice(g * LANES, (g + 1) * LANES)

            def keep(values, row, local=local):
                piece = slice(row, row + PIECE)
                values_ref[t, piece, local] = values
                loaded_ref[slot, piece, local] = (
                    values.astype(F32) * scale_ref[slot, piece, local]
                ).astype(BF16)

            conv_lanes(
                x_ref, rim_ref, weight_ref, bias_ref, span_ref.at[slot * GROUPS + g], lane, keep
            )
        values_copy(t).start()

    def finish(t, slot):
        state = dot(inputs_ref[...], loaded_ref[slot])
        for g in range(GROUPS):
            first = t * GROUPS + g
            part = state[:, g * LANES : (g + 1) * LANES]
            held_ref[pl.ds(first, PAIRS, stride=ROWS), :] = part[0:PAIRS]
            held_ref[pl.ds(first + HALF_GROUPS, PAIRS, stride=ROWS), :] = part[PAIRS:]

    load(0, 0)

    def step(pair, _):
        load(2 * pair + 1, 1)
        finish(2 * pair, 0)
        load(2 * pair + 2, 0)
        finish(2 * pair + 1, 1)
        return 0

    lax.fori_loop(0, HALF_TILES // 2, step, 0)
    finish(HALF_TILES - 1, 0)
    state_ref[:, ROWS:, :] = jnp.broadcast_to(tail_ref[...][None], (PAIRS, 8, LANES)).astype(BF16)

    def move(n, _):
        first = pl.multiple_of(n * ROWS, 8)
        state_ref[n, 0:ROWS, :] = held_ref[pl.ds(first, ROWS), :].astype(BF16)
        return 0

    lax.fori_loop(0, PAIRS, move, 0, unroll=8)
    if own:
        state_copy = pltpu.make_async_copy(state_ref, spare_hbm, sems.at[HALF_TILES])
        state_copy.start()
    for t in range(HALF_TILES):
        values_copy(t).wait()
    if own:
        state_copy.wait()


def far_state_kernel(
    x_ref, rim_ref, weight_ref, bias_ref, to_end_ref, tail_ref,
    values_hbm, state_ref, side_ref, inputs_ref, span_ref, *scratch,
):
    side_values(x_ref, rim_ref, weight_ref, bias_ref, span_ref, side_ref, inputs_ref)
    state_kernel(
        False, x_ref, rim_ref, weight_ref, bias_ref, to_end_ref, tail_ref, inputs_ref,
        values_hbm, state_ref, span_ref, *scratch,
    )


def rows_of_heads(count, core):
    row = lax.rem(iota((count, ROWS, LANES), 1), HALF_GROUPS)
    head = iota((count, ROWS, LANES), 2)
    return (head // 2 == row + core * HALF_GROUPS).astype(F32)


def lanes_of_heads():
    head = iota((2 * LANES, LANES), 0)
    return (lax.rem(head, 2) == iota((2 * LANES, LANES), 1) // HEAD_DIM).astype(F32).astype(BF16)


def decay_rows(high, middle, count, core):
    mask = rows_of_heads(count, core)
    both = jnp.concatenate([mask * high, mask * middle], axis=2).astype(BF16)
    return dot(both.reshape(count * ROWS, 2 * LANES), lanes_of_heads())


def join_kernel(mine_ref, got_ref, out_ref, got_hbm, sem):
    core = core_index()
    copy = pltpu.make_async_copy(got_ref, got_hbm, sem)
    copy.start()

    def join(first_ref, second_ref):
        first = first_ref[0, ROWS:, :].astype(F32)
        second = second_ref[0, ROWS:, :].astype(F32)
        decay = decay_rows(second[None, 0:1, :], second[None, 1:2, :], 1, core)
        whole = (first[0:1] + first[1:2] + first[2:3]) * (second[0:1] + second[1:2] + second[2:3])
        out_ref[:, ROWS:, :] = jnp.broadcast_to(thirds(whole)[None], (PAIRS, 8, LANES)).astype(BF16)

        def step(n, _):
            out_ref[n, 0:ROWS, :] = (
                decay * first_ref[n, 0:ROWS, :].astype(F32) + second_ref[n, 0:ROWS, :].astype(F32)
            ).astype(BF16)
            return 0

        lax.fori_loop(0, PAIRS, step, 0, unroll=4)

    pl.when(core == 0)(lambda: join(mine_ref, got_ref))
    pl.when(core == 1)(lambda: join(got_ref, mine_ref))
    copy.wait()


def scan_kernel(count, pieces_ref, out_ref, decay_ref):
    tails = pieces_ref[:, ROWS:, :].astype(F32)
    decay_ref[...] = decay_rows(tails[:, 0:1, :], tails[:, 1:2, :], count, core_index())

    def step(i, running):
        out_ref[i] = running.astype(BF16)
        piece = pieces_ref[i, 0:ROWS, :].astype(F32)
        return decay_ref[pl.ds(pl.multiple_of(i * ROWS, 8), ROWS), :] * running + piece

    lax.fori_loop(0, count, step, jnp.zeros((ROWS, LANES), F32), unroll=4)


def unpack(state_ref, held_ref):
    def move(n, _):
        first = pl.multiple_of(n * ROWS, 8)
        held_ref[pl.ds(first, ROWS), :] = state_ref[n, 0:ROWS, :].astype(F32)
        return 0

    lax.fori_loop(0, PAIRS, move, 0, unroll=8)


def state_tile(held_ref, t):
    parts = []
    for g in range(GROUPS):
        first = t * GROUPS + g
        parts.append(
            jnp.concatenate(
                [
                    held_ref[pl.ds(first, PAIRS, stride=ROWS), :],
                    held_ref[pl.ds(first + HALF_GROUPS, PAIRS, stride=ROWS), :],
                ],
                axis=0,
            )
        )
    return jnp.concatenate(parts, axis=1)


def factor_values(
    side_ref, dt_ref, log_ref, first_decay, skip_ref,
    both_ref, inputs_ref, factors_ref, halves_ref, rise_ref,
):
    side = side_ref[...]
    inputs_ref[...] = side[:, 0:N_STATE].astype(F32).T.astype(BF16)
    rows, cols = iota((CHUNK, CHUNK), 0), iota((CHUNK, CHUNK), 1)
    before = jnp.zeros((1, HEADS), F32)
    for q in range(CHUNKS):
        span = slice(q * CHUNK, (q + 1) * CHUNK)
        readout = side[span, N_STATE:]
        scores = dot_nt(readout, side[span, 0:N_STATE])
        both_ref[span, 0:CHUNK] = jnp.where(rows >= cols, scores, 0.0).astype(BF16)
        both_ref[span, CHUNK:] = readout
        cumulative, steps = running_decay(log_ref, dt_ref, q)
        total = cumulative[CHUNK - 1 :, :]
        middle = 0.5 * total
        factors_ref[span, 0 : 2 * LANES] = split_pair(
            pad_heads(jnp.exp(middle - cumulative) * steps)
        )
        factors_ref[span, 2 * LANES :] = split_pair(pad_heads(jnp.exp(cumulative - middle)))
        rise_ref[span, :] = split_pair(pad_heads(jnp.exp(cumulative + before) * first_decay))
        before = before + total
        halves_ref[8 * q : 8 * q + 8, :] = split_pair(
            jnp.broadcast_to(pad_heads(jnp.exp(middle)), (8, LANES))
        )
    halves_ref[8 * CHUNKS :, :] = split_pair(jnp.broadcast_to(pad_heads(skip_ref[...]), (8, LANES)))


def far_local_kernel(*refs):
    local_kernel(False, None, *refs)


def own_local_kernel(
    values_hbm, side_ref, dt_ref, log_ref, skip_ref, start_hbm,
    part_hbm, both_ref, inputs_ref, factors_ref, halves_ref, rise_ref,
    *scratch,
):
    def prepare(start_ref):
        tail = start_ref[0, ROWS:, 0:HEADS].astype(F32)
        first_decay = jnp.where(core_index() == 0, 1.0, tail[0:1] + tail[1:2] + tail[2:3])
        factor_values(
            side_ref, dt_ref, log_ref, first_decay, skip_ref,
            both_ref, inputs_ref, factors_ref, halves_ref, rise_ref,
        )

    local_kernel(
        True, prepare, values_hbm, both_ref, inputs_ref, factors_ref, halves_ref, start_hbm,
        part_hbm, *scratch,
    )


def local_kernel(
    own, prepare, values_hbm, both_ref, inputs_ref, factors_ref, halves_ref, start_hbm,
    part_hbm,
    held_ref, scaled_ref, start_ref, values_ref, part_ref, scale_ref, rise_ref, in_sems, out_sems,
):
    half = half_of(own)
    start_copy = pltpu.make_async_copy(start_hbm, start_ref, in_sems.at[HALF_TILES])
    start_copy.start()

    def values_copy(t):
        return pltpu.make_async_copy(
            values_hbm.at[:, t * TILE : (t + 1) * TILE], values_ref.at[t], in_sems.at[t]
        )

    def part_copy(t):
        return pltpu.make_async_copy(
            part_ref.at[t], part_hbm.at[:, t * TILE : (t + 1) * TILE], out_sems.at[t]
        )

    for t in range(HALF_TILES):
        values_copy(t).start()
    start_copy.wait()
    if own:
        prepare(start_ref)

    @pl.when(core_index() == 0)
    def _():
        held_ref[...] = jnp.zeros_like(held_ref)

    pl.when(core_index() == 1)(lambda: unpack(start_ref, held_ref))
    for t in range(HALF_TILES):
        wide = spread(half * HALF_TILES + t)
        halves = dot(halves_ref[...], wide)
        skips = halves[8 * CHUNKS : 8 * CHUNKS + 1, :]
        state = state_tile(held_ref, t)
        values_copy(t).wait()
        scale_ref[...] = dot(factors_ref[:, 0 : 2 * LANES], wide)
        rise_ref[...] = dot(factors_ref[:, 2 * LANES :], wide)
        for q in range(CHUNKS):
            span = slice(q * CHUNK, (q + 1) * CHUNK)
            values = values_ref[t, span, :].astype(F32)
            scaled_ref[q] = (values * scale_ref[span, :]).astype(BF16)
            step = halves[8 * q : 8 * q + 1, :]
            begin = step * state
            mixed = dot(
                both_ref[span, :], jnp.concatenate([scaled_ref[q], begin.astype(BF16)], axis=0)
            )
            part_ref[t, span, :] = (
                mixed * rise_ref[span, :] + skips * values
            )
            if q < CHUNKS - 1:
                state = step * (begin + dot(inputs_ref[:, span], scaled_ref[q]))
        part_copy(t).start()
    for t in range(HALF_TILES):
        part_copy(t).wait()


def mix_kernel(
    own, part_hbm, side_ref, rise_ref, start_ref, *rest
):
    out_hbm, held_ref, part_ref, ready_ref, in_sems, out_sems = rest[-6:]
    half = half_of(own)

    def part_copy(t):
        return pltpu.make_async_copy(
            part_hbm.at[:, t * TILE : (t + 1) * TILE], part_ref.at[t], in_sems.at[t]
        )

    def out_copy(t):
        lanes = pl.ds(pl.multiple_of(half * (INNER // 2) + t * TILE, TILE), TILE)
        return pltpu.make_async_copy(ready_ref.at[t], out_hbm.at[:, lanes], out_sems.at[t])

    for t in range(HALF_TILES):
        part_copy(t).start()
    unpack(start_ref, held_ref)
    for t in range(HALF_TILES):
        wide = spread(half * HALF_TILES + t)
        state = state_tile(held_ref, t).astype(BF16)
        part_copy(t).wait()
        for q in range(CHUNKS):
            span = slice(q * CHUNK, (q + 1) * CHUNK)
            carried = dot(side_ref[span, N_STATE:], state)
            ready_ref[t, span, :] = (
                part_ref[t, span, :] + dot(rise_ref[span, :], wide) * carried
            ).astype(BF16)
        out_copy(t).start()
    for t in range(HALF_TILES):
        out_copy(t).wait()


VMEM = pl.BlockSpec(memory_space=pltpu.VMEM)
HBM = pl.BlockSpec(memory_space=pltpu.HBM)


def params(limit):
    return pltpu.CompilerParams(vmem_limit_bytes=limit * MIB)


def in_hbm(value):
    return pltpu.with_memory_space_constraint(value, pltpu.HBM)


def body(xbc, conv_weight, conv_bias, dt, decay_log, skip):
    count = lax.axis_size(ALL)
    chips = count // 2
    swap = [(i, i ^ 1) for i in range(lax.axis_size("narrow"))]
    onward = [(i, i + 1) for i in range(0, lax.axis_size("narrow"), 2)]
    groups = [[2 * c + k for c in range(chips)] for k in range(2)]
    state_out = pltpu.VMEM((PAIRS, SENT, LANES), BF16)
    state_hbm = pltpu.HBM((PAIRS, SENT, LANES), BF16)
    half_out = pltpu.HBM((TOK, INNER // 2), BF16)
    held = pltpu.VMEM((PAIRS * ROWS, LANES), F32)
    tiles_16 = pltpu.VMEM((HALF_TILES, TOK, TILE), BF16)
    tiles_32 = pltpu.VMEM((HALF_TILES, TOK, TILE), F32)
    tile_sems = pltpu.SemaphoreType.DMA((HALF_TILES,))
    inputs_out = jax.ShapeDtypeStruct((N_STATE, TOK), BF16)
    pair_out = jax.ShapeDtypeStruct((TOK, 2 * LANES), BF16)

    rim = lax.ppermute(xbc[TOK - 8 :], ALL, [(i, i + 1) for i in range(count - 1)])
    x_near, to_end, tail = pl.pallas_call(
        fetch_kernel,
        in_specs=[HBM, VMEM, VMEM],
        out_specs=[VMEM] * 3,
        out_shape=[pltpu.VMEM((TOK, WIDTH), BF16), pair_out, pltpu.VMEM((8, LANES), F32)],
        scratch_shapes=[pltpu.SemaphoreType.DMA],
        compiler_params=params(8),
        name="fetch",
    )(in_hbm(xbc), in_hbm(dt), in_hbm(decay_log))
    bias = conv_bias[None, :]
    state_scratch = [
        pltpu.VMEM((2 * GROUPS, 8 + TOK, LANES), F32),
        held,
        pltpu.VMEM((2, TOK, TILE), F32),
        pltpu.VMEM((2, TOK, TILE), BF16),
        tiles_16,
        pltpu.SemaphoreType.DMA((HALF_TILES + 1,)),
    ]
    values_far, other, side, inputs = pl.pallas_call(
        far_state_kernel,
        in_specs=[VMEM] * 6,
        out_specs=[HBM, VMEM, VMEM, VMEM],
        out_shape=[half_out, state_out, pair_out, inputs_out],
        scratch_shapes=state_scratch,
        compiler_params=params(16),
        name="far_states",
    )(x_near, rim, conv_weight, bias, to_end, tail)
    got = lax.ppermute(other, "narrow", swap)
    x_near, other = lax.optimization_barrier((x_near, other))
    values_own, mine, spare = pl.pallas_call(
        lambda *refs: state_kernel(True, *refs),
        in_specs=[VMEM] * 7,
        out_specs=[HBM, VMEM, HBM],
        out_shape=[half_out, state_out, state_hbm],
        scratch_shapes=state_scratch,
        compiler_params=params(16),
        cost_estimate=pl.CostEstimate(flops=2 * 10**9, bytes_accessed=10**7, transcendentals=0),
        name="own_states",
    )(x_near, rim, conv_weight, bias, to_end, tail, inputs)
    got, mine = lax.optimization_barrier((got, mine))
    joined, got = pl.pallas_call(
        join_kernel,
        in_specs=[VMEM] * 2,
        out_specs=[VMEM, HBM],
        out_shape=[jax.ShapeDtypeStruct((PAIRS, SENT, LANES), BF16), state_hbm],
        scratch_shapes=[pltpu.SemaphoreType.DMA],
        compiler_params=params(8),
        name="join_cores",
    )(mine, got)
    pieces = lax.all_to_all(joined, ALL, 0, 0, axis_index_groups=groups, tiled=True)
    joined, side = lax.optimization_barrier((joined, side))
    local_scratch = [
        held,
        pltpu.VMEM((CHUNKS, CHUNK, TILE), BF16),
        pltpu.VMEM((PAIRS, SENT, LANES), BF16),
        tiles_16,
        tiles_32,
        pltpu.VMEM((TOK, TILE), F32),
        pltpu.VMEM((TOK, TILE), F32),
        pltpu.SemaphoreType.DMA((HALF_TILES + 1,)),
        tile_sems,
    ]
    part_out = pltpu.HBM((TOK, INNER // 2), F32)
    part_own, both, inputs, factors, halves, rise = pl.pallas_call(
        own_local_kernel,
        in_specs=[HBM] + [VMEM] * 4 + [HBM],
        out_specs=[HBM] + [VMEM] * 5,
        out_shape=[
            part_out,
            pair_out,
            inputs_out,
            jax.ShapeDtypeStruct((TOK, 4 * LANES), BF16),
            jax.ShapeDtypeStruct((8 * CHUNKS + 8, 2 * LANES), BF16),
            pair_out,
        ],
        scratch_shapes=local_scratch,
        compiler_params=params(22),
        cost_estimate=pl.CostEstimate(flops=10**6, bytes_accessed=10**5, transcendentals=0),
        name="own_part",
    )(in_hbm(values_own), side, in_hbm(dt), in_hbm(decay_log), skip[None, :], in_hbm(got))
    pieces, part_own = lax.optimization_barrier((pieces, part_own))
    prefixes = pl.pallas_call(
        lambda *refs: scan_kernel(chips, *refs),
        in_specs=[VMEM],
        out_specs=VMEM,
        out_shape=jax.ShapeDtypeStruct((chips, ROWS, LANES), BF16),
        scratch_shapes=[pltpu.VMEM((chips * ROWS, LANES), F32)],
        compiler_params=params(12),
        name="scan_chips",
    )(pieces)
    own = lax.all_to_all(prefixes, ALL, 0, 0, axis_index_groups=groups, tiled=True)
    prefixes, values_far = lax.optimization_barrier((prefixes, values_far))
    prefixes, spare = lax.optimization_barrier((prefixes, spare))
    before = lax.ppermute(spare, "narrow", onward)
    part_far = pl.pallas_call(
        far_local_kernel,
        in_specs=[HBM] + [VMEM] * 4 + [HBM],
        out_specs=HBM,
        out_shape=part_out,
        scratch_shapes=local_scratch,
        compiler_params=params(22),
        cost_estimate=pl.CostEstimate(flops=10**6, bytes_accessed=10**5, transcendentals=0),
        name="far_part",
    )(in_hbm(values_far), both, inputs, factors, halves, in_hbm(before))
    own, part_far = lax.optimization_barrier((own, part_far))
    across = lax.ppermute(own, "narrow", swap)

    def mix(own, part, start, *out):
        return pl.pallas_call(
            lambda *refs: mix_kernel(own, *refs),
            in_specs=[HBM] + [VMEM] * 3 + [HBM] * len(out),
            out_specs=HBM,
            out_shape=jax.ShapeDtypeStruct((TOK, INNER), BF16),
            scratch_shapes=[held, tiles_32, tiles_16, tile_sems, tile_sems],
            input_output_aliases={4: 0} if out else {},
            compiler_params=params(16),
            cost_estimate=pl.CostEstimate(
                flops=10**9, bytes_accessed=10**7, transcendentals=0
            ),
            name="own_mix" if own else "far_mix",
        )(in_hbm(part), side, rise, start, *out)

    out = mix(True, part_own, own)
    across, out = lax.optimization_barrier((across, out))
    return mix(False, part_far, across, out)


def solution(mesh):
    placed = (P(ALL, None), P(), P(), P(None, ALL), P(None, ALL), P())
    return jax.shard_map(
        body, mesh=mesh, in_specs=placed, out_specs=P(ALL, None), check_vma=False
    )
```

time: 697 us -> 81.4 us (0.12)
  waiting for transfers between devices: 348 us -> 7.59 us
  other arithmetic: 150 us -> 0 us
  local copies, waits for them, and re-layouts: 95.2 us -> 2.58 us
  blocking collectives: 45 us -> 0 us
  Pallas kernels: 0 us -> 44.9 us
  matrix products: 38 us -> 0 us
  starting transfers between devices: 4.6 us -> 25.5 us
  between operations: 14 us -> 0.35 us
    all_gather x2 -> x0, waiting for transfers between devices: 282 us -> none  [prefix_2(): pieces = jax.tree.map(lambda part: lax.all_gather(part, axis), value)]
    select_n x22 -> x0, other arithmetic: 97 us -> none  [step(): jnp.where(position < mine, new, old)]
    psum x1 -> x0, waiting for transfers between devices: 66 us -> none  [from_root(): return lax.psum(jnp.where(mine, shard, jnp.zeros_like(shard)), axis)]
    pallas_call x0 -> x9, Pallas kernels: none -> 44.9 us  [the longest x1 10.2 us: body(): pl.pallas_call(own_local_kernel, in_specs=[HBM] + [VMEM] * 4 + [HBM], out...]
    convert_element_type x5 -> x0, local copies, waits for them, and re-layouts: 43.5 us -> none  [the longest x2 31.5 us: body(): return running.reshape(length_dev, INNER).astype(jnp.bfloat16)]
    dot_general x7 -> x0, matrix products: 38 us -> none  [the longest x2 13.4 us: block_local(): jnp.einsum('hts,shp->thp', weights, values, preferred_element_type=jnp.fl...]
    convert_element_type x5 -> x0, other arithmetic: 37.4 us -> none  [the longest x1 14.2 us: convolve(): return jax.nn.silu(running).astype(jnp.bfloat16)]
    all_gather x1 -> x0, blocking collectives: 18.6 us -> none  [prefix_2(): pieces = jax.tree.map(lambda part: lax.all_gather(part, axis), value)]
  transfers between devices with their start and end apart: 4 -> 6, of which waited for: 3 -> 2; matrix products, arithmetic and copies ran while one was open for 3% -> 1% of each run, Pallas kernels for 0% -> 41%
where the time goes in v2:
time: 81.4 us; the launch traced here: 80.9 us
  Pallas kernels  44.9 us (55%)
  starting transfers between devices  25.5 us (31%)
  waiting for transfers between devices  7.59 us (9%)
  local copies, waits for them, and re-layouts  2.58 us (3%)
    all_to_all x1, starting transfers between devices, body(): lax.all_to_all(joined, ALL, 0, 0, axis_index_groups=groups, tiled=True)  10.8 us
    pallas_call x1, Pallas kernels, body(): pl.pallas_call(own_local_kernel, in_specs=[HBM] + [VMEM] * 4 + [HBM], out...  10.2 us
    pallas_call x2, Pallas kernels, mix(): pl.pallas_call(lambda *refs: mix_kernel(own, *refs), in_specs=[HBM] + [VM...  8.82 us
    pallas_call x1, Pallas kernels, body(): pl.pallas_call(far_local_kernel, in_specs=[HBM] + [VMEM] * 4 + [HBM], out...  8.19 us
    all_to_all x1, starting transfers between devices, body(): lax.all_to_all(prefixes, ALL, 0, 0, axis_index_groups=groups, tiled=True)  6.24 us
    pallas_call x1, Pallas kernels, body(): pl.pallas_call(lambda *refs: state_kernel(True, *refs), in_specs=[VMEM] *...  5.39 us
    pallas_call x1, Pallas kernels, body(): pl.pallas_call(far_state_kernel, in_specs=[VMEM] * 6, out_specs=[HBM, VME...  5.31 us
    ppermute x1, starting transfers between devices, body(): lax.ppermute(xbc[TOK - 8:], ALL, [(i, i + 1) for i in range(count - 1)])  4.5 us
  transfers between devices with their start and end apart: 6, of which 2 were waited for; matrix products, arithmetic and copies ran while one was open for 1% of the time, Pallas kernels for 41%

profile of v2, /device:TPU:1, one launch (start us, length us, event | category | flops | bytes accessed | tf_op | source)
XLA Modules:
  0.0 80.9 jit_solution(6626816327034487028)
XLA Ops:
  0.0 0.0 copy-start
  0.0 0.9 %slice.3 = bf16[8,5376]{1,0:T(8,128)(2,1)S(1)} slice(bf16[512,5376]{1,0:T(8,128)(2,1)} %x_hbm.1), slice={[504:512], [0:5376]} | slice | bytes 172032 | tf_op jit(solution)/shard_map/slice | solution.py:461
  0.9 4.5 %collective-permute-start = (bf16[8,5376]{1,0:T(8,128)(2,1)S(1)}, bf16[8,5376]{1,0:T(8,128)(2,1)S(1)}, u32[]{:S(2)}, u32[]{:S(2)}) collective-permute-start(bf16[8,5376]{1,0:T(8,128)(2,1)S(1)} %slice.3), channel_id=1, source_target_pairs={{0,1},{1,2},{2,3},{3,4},{4,5},{5,6},{6,7},{7,8},{8,9},{9,10},{10,1... | collective-permute-start | bytes 258056 | tf_op jit(solution)/shard_map/ppermute | solution.py:461
  5.4 0.8 broadcast_in_dim.6.bias_ref.refs_3_
  6.2 3.6 %fetch.1 = (bf16[512,5376]{1,0:T(8,128)(2,1)S(1)}, bf16[512,256]{1,0:T(8,128)(2,1)S(1)}, f32[8,128]{1,0:T(8,128)S(1)}) custom-call(bf16[512,5376]{1,0:T(8,128)(2,1)} %x_hbm.1, f32[80,512]{1,0:T(8,128)} %dt_ref.3, f32[80,512]{1,0:T(8,128)} %log_ref.3), custom_call_target="tpu_custom_call" | custom-call | tf_op jit(solution)/shard_map/fetch/pallas_call | solution.py:462
  9.8 0.0 collective-permute-done.rim_ref.refs_1_
  9.8 0.0 copy-done
  9.8 5.3 %far_states.1 = (bf16[512,2560]{1,0:T(8,128)(2,1)}, bf16[64,48,128]{2,1,0:T(8,128)(2,1)S(1)}, bf16[512,256]{1,0:T(8,128)(2,1)S(1)}, bf16[128,512]{1,0:T(8,128)(2,1)S(1)}) custom-call(bf16[512,5376]{1,0:T(8,128)(2,1)S(1)} %get-tuple-element.38.x_ref.refs_0_, bf16[8,5376]{1,0:T(8,128)(2,1)S(1)} %collective-permute-done.rim_ref.refs_1_, f32[4,5376]{1,0:T(4,128)S(1)} %copy-done, ...), custom_call_target="tpu_custom_call" | custom-call | tf_op jit(solution)/shard_map/far_states/pallas_call | solution.py:480
  15.1 0.1 collective-permute-start.1
  15.2 0.0 copy-start.1
  15.2 5.4 %own_states.1 = (bf16[512,2560]{1,0:T(8,128)(2,1)}, bf16[64,48,128]{2,1,0:T(8,128)(2,1)S(1)}, bf16[64,48,128]{2,1,0:T(8,128)(2,1)}) custom-call(bf16[512,5376]{1,0:T(8,128)(2,1)S(1)} %get-tuple-element.38.x_ref.refs_0_, bf16[8,5376]{1,0:T(8,128)(2,1)S(1)} %collective-permute-done.rim_ref.refs_1_, f32[4,5376]{1,0:T(4,128)S(1)} %copy-done, ...), custom_call_target="tpu_custom_call" | custom-call | flops 2000000000 | bytes 10000000 | tf_op jit(solution)/shard_map/own_states/pallas_call | solution.py:491
  20.6 0.0 collective-permute-done.1.got_ref
  20.6 1.9 %join_cores.1 = (bf16[64,48,128]{2,1,0:T(8,128)(2,1)}, bf16[64,48,128]{2,1,0:T(8,128)(2,1)}) custom-call(bf16[64,48,128]{2,1,0:T(8,128)(2,1)S(1)} %get-tuple-element.41.mine_ref, bf16[64,48,128]{2,1,0:T(8,128)(2,1)S(1)} %collective-permute-done.1.got_ref), custom_call_target="tpu_custom_call" | custom-call | tf_op jit(solution)/shard_map/join_cores/pallas_call | solution.py:502
  22.5 10.8 %all-to-all-start = ((bf16[64,48,128]{2,1,0:T(8,128)(2,1)}), bf16[64,48,128]{2,1,0:T(8,128)(2,1)S(1)}, u32[]{:S(2)}, u32[]{:S(2)}) async-start(bf16[64,48,128]{2,1,0:T(8,128)(2,1)} %get-tuple-element.43), calls=%async_computation | async-start | bytes 1572864 | tf_op jit(solution)/shard_map/all_to_all | solution.py:511
  33.4 1.3 %collective-permute-start.2 = (bf16[64,48,128]{2,1,0:T(8,128)(2,1)}, bf16[64,48,128]{2,1,0:T(8,128)(2,1)S(1)}, u32[]{:S(2)}, u32[]{:S(2)}) collective-permute-start(bf16[64,48,128]{2,1,0:T(8,128)(2,1)} %get-tuple-element.56), channel_id=1, source_target_pairs={{0,1},{2,3},{4,5},{6,7},{8,9},{10,11},{12,13},{14,15},{16,17},{18,... | collective-permute-start | bytes 2359304 | tf_op jit(solution)/shard_map/ppermute | solution.py:555
  34.7 0.0 copy-done.1
  34.7 10.2 %own_part.1 = (f32[512,2560]{1,0:T(8,128)}, bf16[512,256]{1,0:T(8,128)(2,1)S(1)}, bf16[128,512]{1,0:T(8,128)(2,1)S(1)}, bf16[512,512]{1,0:T(8,128)(2,1)S(1)}, bf...) custom-call(bf16[512,2560]{1,0:T(8,128)(2,1)} %get-tuple-element.44.values_hbm, ...), custom_call_target="tpu_custom_call" | custom-call | flops 1000000 | bytes 100000 | tf_op jit(solution)/shard_map/own_part/pallas_call | solution.py:525
  44.9 3.6 %all-to-all-done.refs_0_ = bf16[64,48,128]{2,1,0:T(8,128)(2,1)S(1)} async-done(((bf16[64,48,128]{2,1,0:T(8,128)(2,1)}), bf16[64,48,128]{2,1,0:T(8,128)(2,1)S(1)}, u32[]{:S(2)}, u32[]{:S(2)}) %all-to-all-start) | async-done | bytes 786464 | tf_op jit(solution)/shard_map/all_to_all | solution.py:511
  48.4 1.5 %scan_chips.1 = bf16[64,40,128]{2,1,0:T(8,128)(2,1)} custom-call(bf16[64,48,128]{2,1,0:T(8,128)(2,1)S(1)} %all-to-all-done.refs_0_), custom_call_target="tpu_custom_call" | custom-call | tf_op jit(solution)/shard_map/scan_chips/pallas_call | solution.py:543
  50.0 6.2 %all-to-all-start.1 = ((bf16[64,40,128]{2,1,0:T(8,128)(2,1)}), bf16[64,40,128]{2,1,0:T(8,128)(2,1)S(1)}, u32[]{:S(2)}, u32[]{:S(2)}) async-start(bf16[64,40,128]{2,1,0:T(8,128)(2,1)} %scan_chips.1), calls=%async_computation.1 | async-start | bytes 1310720 | tf_op jit(solution)/shard_map/all_to_all | solution.py:552
  56.2 0.0 collective-permute-done.2.refs_5_
  56.2 0.0 copy-start.2
  56.2 0.9 %copy-done.2 = bf16[64,48,128]{2,1,0:T(8,128)(2,1)} copy-done((bf16[64,48,128]{2,1,0:T(8,128)(2,1)}, bf16[64,48,128]{2,1,0:T(8,128)(2,1)S(1)}, u32[]{:S(2)}) %copy-start.2) | copy-done | bytes 786456
  57.1 8.2 %far_part.1.refs_0_ = f32[512,2560]{1,0:T(8,128)} custom-call(bf16[512,2560]{1,0:T(8,128)(2,1)} %get-tuple-element.51.refs_0_, bf16[512,256]{1,0:T(8,128)(2,1)S(1)} %get-tuple-element.52.refs_1_, bf16[128,512]{1,0:T(8,128)(2,1)S(1)} %get-tuple-element.53.refs_2_, bf16[512,512]{1,0:T(8,128)(2,1)S(1)} %get-tuple-element.54.refs_3_, ...), custom_call_target="tpu_custom_call" | custom-call | flops 1000000 | bytes 100000 | tf_op jit(solution)/shard_map/far_part/pallas_call | solution.py:556
  65.3 4.0 %all-to-all-done.1.refs_3_ = bf16[64,40,128]{2,1,0:T(8,128)(2,1)S(1)} async-done(((bf16[64,40,128]{2,1,0:T(8,128)(2,1)}), bf16[64,40,128]{2,1,0:T(8,128)(2,1)S(1)}, u32[]{:S(2)}, u32[]{:S(2)}) %all-to-all-start.1) | async-done | bytes 655392 | tf_op jit(solution)/shard_map/all_to_all | solution.py:552
  69.4 2.6 %collective-permute-start.3 = (bf16[64,40,128]{2,1,0:T(8,128)(2,1)S(1)}, bf16[64,40,128]{2,1,0:T(8,128)(2,1)S(1)}, u32[]{:S(2)}, u32[]{:S(2)}) collective-permute-start(bf16[64,40,128]{2,1,0:T(8,128)(2,1)S(1)} %all-to-all-done.1.refs_3_), channel_id=1, source_target_pairs={{0,1},{1,0},{2,3},{3,2},{4,5},{5,4},{6,7},{7,6},{8,9},{9,8},{10,11... | collective-permute-start | bytes 1966088 | tf_op jit(solution)/shard_map/ppermute | solution.py:567
  71.9 4.4 %own_mix.1.refs_4_ = bf16[512,5120]{1,0:T(8,128)(2,1)} custom-call(f32[512,2560]{1,0:T(8,128)} %get-tuple-element.60.refs_0_, bf16[512,256]{1,0:T(8,128)(2,1)S(1)} %get-tuple-element.46.side_ref.refs_1_, bf16[512,256]{1,0:T(8,128)(2,1)S(1)} %get-tuple-element.58.refs_2_, bf16[64,40,128]{2,1,0:T(8,128)(2,1)S(1)} %all-to-all-done.1.refs_3_), custom_call_target="tpu_custom_call" | custom-call | flops 1000000000 | bytes 10000000 | tf_op jit(solution)/shard_map/own_mix/pallas_call | solution.py:570
  76.3 0.0 collective-permute-done.3.refs_3_
  76.3 4.4 %far_mix.1 = bf16[512,5120]{1,0:T(8,128)(2,1)} custom-call(f32[512,2560]{1,0:T(8,128)} %far_part.1.refs_0_, bf16[512,256]{1,0:T(8,128)(2,1)S(1)} %get-tuple-element.46.side_ref.refs_1_, bf16[512,256]{1,0:T(8,128)(2,1)S(1)} %get-tuple-element.58.refs_2_, bf16[64,40,128]{2,1,0:T(8,128)(2,1)S(1)} %collective-permute-done.3.refs_3_, ...), custom_call_target="tpu_custom_call", output_to_operand_aliasing={{}: (4, {})} | custom-call | flops 1000000000 | bytes 10000000 | tf_op jit(solution)/shard_map/far_mix/pallas_call | solution.py:570
Async XLA Ops:
  0.0 9.8 %copy-start = (f32[4,5376]{1,0:T(4,128)S(1)}, f32[4,5376]{1,0:T(4,128)}, u32[]{:S(2)}) copy-start(f32[4,5376]{1,0:T(4,128)} %refs_2_.1) | copy-start | bytes 258052
  0.9 8.8 %collective-permute-start = (bf16[8,5376]{1,0:T(8,128)(2,1)S(1)}, bf16[8,5376]{1,0:T(8,128)(2,1)S(1)}, u32[]{:S(2)}, u32[]{:S(2)}) collective-permute-start(bf16[8,5376]{1,0:T(8,128)(2,1)S(1)} %slice.3), channel_id=1, source_target_pairs={{0,1},{1,2},{2,3},{3,4},{4,5},{5,6},{6,7},{7,8},{8,9},{9,10},{10,1... | collective-permute-start | bytes 258056 | tf_op jit(solution)/shard_map/ppermute | solution.py:461
  15.1 5.5 %collective-permute-start.1 = (bf16[64,48,128]{2,1,0:T(8,128)(2,1)S(1)}, bf16[64,48,128]{2,1,0:T(8,128)(2,1)S(1)}, u32[]{:S(2)}, u32[]{:S(2)}) collective-permute-start(bf16[64,48,128]{2,1,0:T(8,128)(2,1)S(1)} %get-tuple-element.37), channel_id=1, source_target_pairs={{0,1},{1,0},{2,3},{3,2},{4,5},{5,4},{6,7},{7,6},{8,9},{9,8},{10,11... | collective-permute-start | bytes 2359304 | tf_op jit(solution)/shard_map/ppermute | solution.py:489
  15.2 19.5 %copy-start.1 = (f32[80]{0:T(128)S(1)}, f32[80]{0:T(128)}, u32[]{:S(2)}) copy-start(f32[80]{0:T(128)} %param.11) | copy-start | bytes 964
  22.5 25.9 %all-to-all-start = ((bf16[64,48,128]{2,1,0:T(8,128)(2,1)}), bf16[64,48,128]{2,1,0:T(8,128)(2,1)S(1)}, u32[]{:S(2)}, u32[]{:S(2)}) async-start(bf16[64,48,128]{2,1,0:T(8,128)(2,1)} %get-tuple-element.43), calls=%async_computation | async-start | bytes 1572864 | tf_op jit(solution)/shard_map/all_to_all | solution.py:511
  33.4 22.9 %collective-permute-start.2 = (bf16[64,48,128]{2,1,0:T(8,128)(2,1)}, bf16[64,48,128]{2,1,0:T(8,128)(2,1)S(1)}, u32[]{:S(2)}, u32[]{:S(2)}) collective-permute-start(bf16[64,48,128]{2,1,0:T(8,128)(2,1)} %get-tuple-element.56), channel_id=1, source_target_pairs={{0,1},{2,3},{4,5},{6,7},{8,9},{10,11},{12,13},{14,15},{16,17},{18,... | collective-permute-start | bytes 2359304 | tf_op jit(solution)/shard_map/ppermute | solution.py:555
  50.0 19.4 %all-to-all-start.1 = ((bf16[64,40,128]{2,1,0:T(8,128)(2,1)}), bf16[64,40,128]{2,1,0:T(8,128)(2,1)S(1)}, u32[]{:S(2)}, u32[]{:S(2)}) async-start(bf16[64,40,128]{2,1,0:T(8,128)(2,1)} %scan_chips.1), calls=%async_computation.1 | async-start | bytes 1310720 | tf_op jit(solution)/shard_map/all_to_all | solution.py:552
  56.2 0.9 %copy-start.2 = (bf16[64,48,128]{2,1,0:T(8,128)(2,1)}, bf16[64,48,128]{2,1,0:T(8,128)(2,1)S(1)}, u32[]{:S(2)}) copy-start(bf16[64,48,128]{2,1,0:T(8,128)(2,1)S(1)} %collective-permute-done.2.refs_5_) | copy-start | bytes 2359300
  69.4 7.0 %collective-permute-start.3 = (bf16[64,40,128]{2,1,0:T(8,128)(2,1)S(1)}, bf16[64,40,128]{2,1,0:T(8,128)(2,1)S(1)}, u32[]{:S(2)}, u32[]{:S(2)}) collective-permute-start(bf16[64,40,128]{2,1,0:T(8,128)(2,1)S(1)} %all-to-all-done.1.refs_3_), channel_id=1, source_target_pairs={{0,1},{1,0},{2,3},{3,2},{4,5},{5,4},{6,7},{7,6},{8,9},{9,8},{10,11... | collective-permute-start | bytes 1966088 | tf_op jit(solution)/shard_map/ppermute | solution.py:567

commit v3 on v2

--- a/solution.py
+++ b/solution.py
@@ -20,6 +20,8 @@
 GROUPS = TILE // LANES
 PIECE = 64
 HALF_TILES = TILES // 2
+HEAD_TILES = 2
+BATCH = 16
 HALF_GROUPS = INNER // LANES // 2
 PAIRS = N_STATE // 2
 ROWS = 2 * HALF_GROUPS
@@ -83,17 +85,36 @@
     return jnp.concatenate([high, middle, low, jnp.zeros((5, LANES), F32)], axis=0)
 
 
-def fetch_kernel(x_hbm, dt_ref, log_ref, x_ref, to_end_ref, tail_ref, sem):
+def fetch_kernel(
+    x_hbm, dt_ref, log_ref, skip_ref,
+    x_ref, to_end_ref, tail_ref, factors_ref, halves_ref, level_ref, sem,
+):
     copy = pltpu.make_async_copy(x_hbm, x_ref, sem)
     copy.start()
+    decays = [running_decay(log_ref, dt_ref, q) for q in range(CHUNKS)]
+    totals = [cumulative[CHUNK - 1 :, :] for cumulative, _ in decays]
     after = jnp.zeros((1, HEADS), F32)
     for q in reversed(range(CHUNKS)):
-        cumulative, steps = running_decay(log_ref, dt_ref, q)
-        total = cumulative[CHUNK - 1 :, :]
-        to_end = jnp.exp(total - cumulative + after) * steps
+        cumulative, steps = decays[q]
+        to_end = jnp.exp(totals[q] - cumulative + after) * steps
         to_end_ref[q * CHUNK : (q + 1) * CHUNK, :] = split_pair(pad_heads(to_end))
-        after = after + total
+        after = after + totals[q]
     tail_ref[...] = thirds(pad_heads(jnp.exp(after)))
+    before = jnp.zeros((1, HEADS), F32)
+    for q in range(CHUNKS):
+        span = slice(q * CHUNK, (q + 1) * CHUNK)
+        cumulative, steps = decays[q]
+        middle = 0.5 * totals[q]
+        factors_ref[span, 0 : 2 * LANES] = split_pair(
+            pad_heads(jnp.exp(middle - cumulative) * steps)
+        )
+        factors_ref[span, 2 * LANES :] = split_pair(pad_heads(jnp.exp(cumulative - middle)))
+        level_ref[span, :] = pad_heads(jnp.exp(cumulative + before))
+        before = before + totals[q]
+        halves_ref[8 * q : 8 * q + 8, :] = split_pair(
+            jnp.broadcast_to(pad_heads(jnp.exp(middle)), (8, LANES))
+        )
+    halves_ref[8 * CHUNKS :, :] = split_pair(jnp.broadcast_to(pad_heads(skip_ref[...]), (8, LANES)))
     copy.wait()
 
 
@@ -111,10 +132,6 @@
         after((half + half * jnp.tanh(half)).astype(BF16), row)
 
 
-def tile_lanes(t):
-    return pl.ds(pl.multiple_of(t * TILE, TILE), TILE)
-
-
 def half_of(own):
     return core_index() if own else 1 - core_index()
 
@@ -141,7 +158,7 @@
 
     def values_copy(t):
         return pltpu.make_async_copy(
-            values_ref.at[t], values_hbm.at[:, tile_lanes(t)], sems.at[t]
+            values_ref.at[t], values_hbm.at[t], sems.at[t]
         )
 
     def load(t, slot):
@@ -226,10 +243,14 @@
     return dot(both.reshape(count * ROWS, 2 * LANES), lanes_of_heads())
 
 
-def join_kernel(mine_ref, got_ref, out_ref, got_hbm, sem):
+def join_kernel(mine_ref, got_ref, out_hbm, got_hbm, out_ref, sems):
     core = core_index()
-    copy = pltpu.make_async_copy(got_ref, got_hbm, sem)
+    copy = pltpu.make_async_copy(got_ref, got_hbm, sems.at[PAIRS // BATCH])
     copy.start()
+
+    def out_copy(batch):
+        some = pl.ds(batch * BATCH, BATCH)
+        return pltpu.make_async_copy(out_ref.at[some], out_hbm.at[some], sems.at[batch])
 
     def join(first_ref, second_ref):
         first = first_ref[0, ROWS:, :].astype(F32)
@@ -244,23 +265,43 @@
             ).astype(BF16)
             return 0
 
-        lax.fori_loop(0, PAIRS, step, 0, unroll=4)
+        def some(batch, _):
+            lax.fori_loop(0, BATCH, lambda i, c: step(batch * BATCH + i, c), 0, unroll=4)
+            out_copy(batch).start()
+            return 0
+
+        lax.fori_loop(0, PAIRS // BATCH, some, 0)
 
     pl.when(core == 0)(lambda: join(mine_ref, got_ref))
     pl.when(core == 1)(lambda: join(got_ref, mine_ref))
+    for batch in range(PAIRS // BATCH):
+        out_copy(batch).wait()
     copy.wait()
 
 
-def scan_kernel(count, pieces_ref, out_ref, decay_ref):
+def scan_kernel(count, pieces_ref, out_hbm, out_ref, decay_ref, sems):
     tails = pieces_ref[:, ROWS:, :].astype(F32)
     decay_ref[...] = decay_rows(tails[:, 0:1, :], tails[:, 1:2, :], count, core_index())
+
+    def out_copy(batch):
+        some = pl.ds(batch * BATCH, BATCH)
+        return pltpu.make_async_copy(out_ref.at[some], out_hbm.at[some], sems.at[batch])
 
     def step(i, running):
         out_ref[i] = running.astype(BF16)
         piece = pieces_ref[i, 0:ROWS, :].astype(F32)
         return decay_ref[pl.ds(pl.multiple_of(i * ROWS, 8), ROWS), :] * running + piece
 
-    lax.fori_loop(0, count, step, jnp.zeros((ROWS, LANES), F32), unroll=4)
+    def some(batch, running):
+        running = lax.fori_loop(
+            0, BATCH, lambda i, held: step(batch * BATCH + i, held), running, unroll=4
+        )
+        out_copy(batch).start()
+        return running
+
+    lax.fori_loop(0, count // BATCH, some, jnp.zeros((ROWS, LANES), F32))
+    for batch in range(count // BATCH):
+        out_copy(batch).wait()
 
 
 def unpack(state_ref, held_ref):
@@ -288,51 +329,40 @@
     return jnp.concatenate(parts, axis=1)
 
 
-def factor_values(
-    side_ref, dt_ref, log_ref, first_decay, skip_ref,
-    both_ref, inputs_ref, factors_ref, halves_ref, rise_ref,
-):
+def shared_scores(side_ref, both_ref):
     side = side_ref[...]
-    inputs_ref[...] = side[:, 0:N_STATE].astype(F32).T.astype(BF16)
     rows, cols = iota((CHUNK, CHUNK), 0), iota((CHUNK, CHUNK), 1)
-    before = jnp.zeros((1, HEADS), F32)
     for q in range(CHUNKS):
         span = slice(q * CHUNK, (q + 1) * CHUNK)
         readout = side[span, N_STATE:]
         scores = dot_nt(readout, side[span, 0:N_STATE])
         both_ref[span, 0:CHUNK] = jnp.where(rows >= cols, scores, 0.0).astype(BF16)
         both_ref[span, CHUNK:] = readout
-        cumulative, steps = running_decay(log_ref, dt_ref, q)
-        total = cumulative[CHUNK - 1 :, :]
-        middle = 0.5 * total
-        factors_ref[span, 0 : 2 * LANES] = split_pair(
-            pad_heads(jnp.exp(middle - cumulative) * steps)
-        )
-        factors_ref[span, 2 * LANES :] = split_pair(pad_heads(jnp.exp(cumulative - middle)))
-        rise_ref[span, :] = split_pair(pad_heads(jnp.exp(cumulative + before) * first_decay))
-        before = before + total
-        halves_ref[8 * q : 8 * q + 8, :] = split_pair(
-            jnp.broadcast_to(pad_heads(jnp.exp(middle)), (8, LANES))
-        )
-    halves_ref[8 * CHUNKS :, :] = split_pair(jnp.broadcast_to(pad_heads(skip_ref[...]), (8, LANES)))
-
-
-def far_local_kernel(*refs):
-    local_kernel(False, None, *refs)
+
+
+def far_local_kernel(
+    values_hbm, part_own_hbm, both_ref, inputs_ref, factors_ref, halves_ref, start_hbm,
+    part_hbm, head_ref, *scratch,
+):
+    copy = pltpu.make_async_copy(part_own_hbm.at[0:HEAD_TILES], head_ref, scratch[-1])
+    copy.start()
+    local_kernel(
+        False, None, values_hbm, both_ref, inputs_ref, factors_ref, halves_ref, start_hbm,
+        part_hbm, *scratch[:-1],
+    )
+    copy.wait()
 
 
 def own_local_kernel(
-    values_hbm, side_ref, dt_ref, log_ref, skip_ref, start_hbm,
-    part_hbm, both_ref, inputs_ref, factors_ref, halves_ref, rise_ref,
+    values_hbm, side_ref, level_ref, inputs_ref, factors_ref, halves_ref, start_hbm,
+    part_hbm, both_ref, rise_ref,
     *scratch,
 ):
     def prepare(start_ref):
-        tail = start_ref[0, ROWS:, 0:HEADS].astype(F32)
+        tail = start_ref[0, ROWS:, :].astype(F32)
         first_decay = jnp.where(core_index() == 0, 1.0, tail[0:1] + tail[1:2] + tail[2:3])
-        factor_values(
-            side_ref, dt_ref, log_ref, first_decay, skip_ref,
-            both_ref, inputs_ref, factors_ref, halves_ref, rise_ref,
-        )
+        rise_ref[...] = split_pair(level_ref[...] * first_decay)
+        shared_scores(side_ref, both_ref)
 
     local_kernel(
         True, prepare, values_hbm, both_ref, inputs_ref, factors_ref, halves_ref, start_hbm,
@@ -351,12 +381,12 @@
 
     def values_copy(t):
         return pltpu.make_async_copy(
-            values_hbm.at[:, t * TILE : (t + 1) * TILE], values_ref.at[t], in_sems.at[t]
+            values_hbm.at[t], values_ref.at[t], in_sems.at[t]
         )
 
     def part_copy(t):
         return pltpu.make_async_copy(
-            part_ref.at[t], part_hbm.at[:, t * TILE : (t + 1) * TILE], out_sems.at[t]
+            part_ref.at[t], part_hbm.at[t], out_sems.at[t]
         )
 
     for t in range(HALF_TILES):
@@ -387,9 +417,7 @@
             mixed = dot(
                 both_ref[span, :], jnp.concatenate([scaled_ref[q], begin.astype(BF16)], axis=0)
             )
-            part_ref[t, span, :] = (
-                mixed * rise_ref[span, :] + skips * values
-            )
+            part_ref[t, span, :] = (mixed * rise_ref[span, :] + skips * values).astype(BF16)
             if q < CHUNKS - 1:
                 state = step * (begin + dot(inputs_ref[:, span], scaled_ref[q]))
         part_copy(t).start()
@@ -397,37 +425,64 @@
         part_copy(t).wait()
 
 
+def own_mix_kernel(
+    head_ref, part_hbm, far_part_hbm, side_ref, rise_ref, start_ref,
+    out_hbm, far_part_ref, held_ref, ready_ref, part_ref, in_sems, out_sems, far_sem,
+):
+    copy = pltpu.make_async_copy(far_part_hbm, far_part_ref, far_sem)
+    mix_kernel(
+        True, head_ref, part_hbm, side_ref, rise_ref, start_ref, out_hbm,
+        held_ref, ready_ref, part_ref, in_sems, out_sems, copy,
+    )
+
+
+def far_mix_kernel(part_ref, side_ref, rise_ref, start_ref, _, *rest):
+    out_hbm, held_ref, ready_ref, out_sems = rest
+    mix_kernel(
+        False, None, None, side_ref, rise_ref, start_ref, out_hbm,
+        held_ref, ready_ref, part_ref, None, out_sems, None,
+    )
+
+
 def mix_kernel(
-    own, part_hbm, side_ref, rise_ref, start_ref, *rest
-):
-    out_hbm, held_ref, part_ref, ready_ref, in_sems, out_sems = rest[-6:]
+    own, head_ref, part_hbm, side_ref, rise_ref, start_ref, out_hbm,
+    held_ref, ready_ref, part_ref, in_sems, out_sems, next_copy,
+):
     half = half_of(own)
 
     def part_copy(t):
         return pltpu.make_async_copy(
-            part_hbm.at[:, t * TILE : (t + 1) * TILE], part_ref.at[t], in_sems.at[t]
+            part_hbm.at[t], part_ref.at[t], in_sems.at[t]
         )
 
     def out_copy(t):
         lanes = pl.ds(pl.multiple_of(half * (INNER // 2) + t * TILE, TILE), TILE)
         return pltpu.make_async_copy(ready_ref.at[t], out_hbm.at[:, lanes], out_sems.at[t])
 
-    for t in range(HALF_TILES):
-        part_copy(t).start()
+    if own:
+        for t in range(HEAD_TILES, HALF_TILES):
+            part_copy(t).start()
+        next_copy.start()
     unpack(start_ref, held_ref)
     for t in range(HALF_TILES):
         wide = spread(half * HALF_TILES + t)
         state = state_tile(held_ref, t).astype(BF16)
-        part_copy(t).wait()
+        tile_ref = part_ref.at[t]
+        if own and t < HEAD_TILES:
+            tile_ref = head_ref.at[t]
+        elif own:
+            part_copy(t).wait()
         for q in range(CHUNKS):
             span = slice(q * CHUNK, (q + 1) * CHUNK)
             carried = dot(side_ref[span, N_STATE:], state)
             ready_ref[t, span, :] = (
-                part_ref[t, span, :] + dot(rise_ref[span, :], wide) * carried
+                tile_ref[span, :].astype(F32) + dot(rise_ref[span, :], wide) * carried
             ).astype(BF16)
         out_copy(t).start()
     for t in range(HALF_TILES):
         out_copy(t).wait()
+    if own:
+        next_copy.wait()
 
 
 VMEM = pl.BlockSpec(memory_space=pltpu.VMEM)
@@ -450,24 +505,30 @@
     groups = [[2 * c + k for c in range(chips)] for k in range(2)]
     state_out = pltpu.VMEM((PAIRS, SENT, LANES), BF16)
     state_hbm = pltpu.HBM((PAIRS, SENT, LANES), BF16)
-    half_out = pltpu.HBM((TOK, INNER // 2), BF16)
+    half_out = pltpu.HBM((HALF_TILES, TOK, TILE), BF16)
     held = pltpu.VMEM((PAIRS * ROWS, LANES), F32)
     tiles_16 = pltpu.VMEM((HALF_TILES, TOK, TILE), BF16)
-    tiles_32 = pltpu.VMEM((HALF_TILES, TOK, TILE), F32)
     tile_sems = pltpu.SemaphoreType.DMA((HALF_TILES,))
     inputs_out = jax.ShapeDtypeStruct((N_STATE, TOK), BF16)
     pair_out = jax.ShapeDtypeStruct((TOK, 2 * LANES), BF16)
 
     rim = lax.ppermute(xbc[TOK - 8 :], ALL, [(i, i + 1) for i in range(count - 1)])
-    x_near, to_end, tail = pl.pallas_call(
+    x_near, to_end, tail, factors, halves, level = pl.pallas_call(
         fetch_kernel,
-        in_specs=[HBM, VMEM, VMEM],
-        out_specs=[VMEM] * 3,
-        out_shape=[pltpu.VMEM((TOK, WIDTH), BF16), pair_out, pltpu.VMEM((8, LANES), F32)],
+        in_specs=[HBM, VMEM, VMEM, VMEM],
+        out_specs=[VMEM] * 6,
+        out_shape=[
+            pltpu.VMEM((TOK, WIDTH), BF16),
+            pair_out,
+            pltpu.VMEM((8, LANES), F32),
+            jax.ShapeDtypeStruct((TOK, 4 * LANES), BF16),
+            jax.ShapeDtypeStruct((8 * CHUNKS + 8, 2 * LANES), BF16),
+            jax.ShapeDtypeStruct((TOK, LANES), F32),
+        ],
         scratch_shapes=[pltpu.SemaphoreType.DMA],
         compiler_params=params(8),
         name="fetch",
-    )(in_hbm(xbc), in_hbm(dt), in_hbm(decay_log))
+    )(in_hbm(xbc), in_hbm(dt), in_hbm(decay_log), skip[None, :])
     bias = conv_bias[None, :]
     state_scratch = [
         pltpu.VMEM((2 * GROUPS, 8 + TOK, LANES), F32),
@@ -502,9 +563,12 @@
     joined, got = pl.pallas_call(
         join_kernel,
         in_specs=[VMEM] * 2,
-        out_specs=[VMEM, HBM],
-        out_shape=[jax.ShapeDtypeStruct((PAIRS, SENT, LANES), BF16), state_hbm],
-        scratch_shapes=[pltpu.SemaphoreType.DMA],
+        out_specs=[HBM, HBM],
+        out_shape=[state_hbm, state_hbm],
+        scratch_shapes=[
+            pltpu.VMEM((PAIRS, SENT, LANES), BF16),
+            pltpu.SemaphoreType.DMA((PAIRS // BATCH + 1,)),
+        ],
         compiler_params=params(8),
         name="join_cores",
     )(mine, got)
@@ -515,37 +579,33 @@
         pltpu.VMEM((CHUNKS, CHUNK, TILE), BF16),
         pltpu.VMEM((PAIRS, SENT, LANES), BF16),
         tiles_16,
-        tiles_32,
+        tiles_16,
         pltpu.VMEM((TOK, TILE), F32),
         pltpu.VMEM((TOK, TILE), F32),
         pltpu.SemaphoreType.DMA((HALF_TILES + 1,)),
         tile_sems,
     ]
-    part_out = pltpu.HBM((TOK, INNER // 2), F32)
-    part_own, both, inputs, factors, halves, rise = pl.pallas_call(
+    part_own, both, rise = pl.pallas_call(
         own_local_kernel,
-        in_specs=[HBM] + [VMEM] * 4 + [HBM],
-        out_specs=[HBM] + [VMEM] * 5,
-        out_shape=[
-            part_out,
-            pair_out,
-            inputs_out,
-            jax.ShapeDtypeStruct((TOK, 4 * LANES), BF16),
-            jax.ShapeDtypeStruct((8 * CHUNKS + 8, 2 * LANES), BF16),
-            pair_out,
-        ],
+        in_specs=[HBM] + [VMEM] * 5 + [HBM],
+        out_specs=[HBM] + [VMEM] * 2,
+        out_shape=[half_out, pair_out, pair_out],
         scratch_shapes=local_scratch,
         compiler_params=params(22),
         cost_estimate=pl.CostEstimate(flops=10**6, bytes_accessed=10**5, transcendentals=0),
         name="own_part",
-    )(in_hbm(values_own), side, in_hbm(dt), in_hbm(decay_log), skip[None, :], in_hbm(got))
+    )(in_hbm(values_own), side, level, inputs, factors, halves, in_hbm(got))
     pieces, part_own = lax.optimization_barrier((pieces, part_own))
     prefixes = pl.pallas_call(
         lambda *refs: scan_kernel(chips, *refs),
         in_specs=[VMEM],
-        out_specs=VMEM,
-        out_shape=jax.ShapeDtypeStruct((chips, ROWS, LANES), BF16),
-        scratch_shapes=[pltpu.VMEM((chips * ROWS, LANES), F32)],
+        out_specs=HBM,
+        out_shape=pltpu.HBM((chips, ROWS, LANES), BF16),
+        scratch_shapes=[
+            pltpu.VMEM((chips, ROWS, LANES), BF16),
+            pltpu.VMEM((chips * ROWS, LANES), F32),
+            pltpu.SemaphoreType.DMA((chips // BATCH,)),
+        ],
         compiler_params=params(12),
         name="scan_chips",
     )(pieces)
@@ -553,37 +613,43 @@
     prefixes, values_far = lax.optimization_barrier((prefixes, values_far))
     prefixes, spare = lax.optimization_barrier((prefixes, spare))
     before = lax.ppermute(spare, "narrow", onward)
-    part_far = pl.pallas_call(
+    part_far, head = pl.pallas_call(
         far_local_kernel,
-        in_specs=[HBM] + [VMEM] * 4 + [HBM],
-        out_specs=HBM,
-        out_shape=part_out,
-        scratch_shapes=local_scratch,
+        in_specs=[HBM] * 2 + [VMEM] * 4 + [HBM],
+        out_specs=[HBM, VMEM],
+        out_shape=[half_out, pltpu.VMEM((HEAD_TILES, TOK, TILE), BF16)],
+        scratch_shapes=local_scratch + [pltpu.SemaphoreType.DMA],
         compiler_params=params(22),
         cost_estimate=pl.CostEstimate(flops=10**6, bytes_accessed=10**5, transcendentals=0),
         name="far_part",
-    )(in_hbm(values_far), both, inputs, factors, halves, in_hbm(before))
+    )(in_hbm(values_far), in_hbm(part_own), both, inputs, factors, halves, in_hbm(before))
     own, part_far = lax.optimization_barrier((own, part_far))
     across = lax.ppermute(own, "narrow", swap)
 
-    def mix(own, part, start, *out):
-        return pl.pallas_call(
-            lambda *refs: mix_kernel(own, *refs),
-            in_specs=[HBM] + [VMEM] * 3 + [HBM] * len(out),
-            out_specs=HBM,
-            out_shape=jax.ShapeDtypeStruct((TOK, INNER), BF16),
-            scratch_shapes=[held, tiles_32, tiles_16, tile_sems, tile_sems],
-            input_output_aliases={4: 0} if out else {},
-            compiler_params=params(16),
-            cost_estimate=pl.CostEstimate(
-                flops=10**9, bytes_accessed=10**7, transcendentals=0
-            ),
-            name="own_mix" if own else "far_mix",
-        )(in_hbm(part), side, rise, start, *out)
-
-    out = mix(True, part_own, own)
+    out_type = jax.ShapeDtypeStruct((TOK, INNER), BF16)
+    out, part_far = pl.pallas_call(
+        own_mix_kernel,
+        in_specs=[VMEM] + [HBM] * 2 + [VMEM] * 3,
+        out_specs=[HBM, VMEM],
+        out_shape=[out_type, pltpu.VMEM((HALF_TILES, TOK, TILE), BF16)],
+        scratch_shapes=[
+            held, tiles_16, tiles_16, tile_sems, tile_sems, pltpu.SemaphoreType.DMA
+        ],
+        compiler_params=params(16),
+        cost_estimate=pl.CostEstimate(flops=10**9, bytes_accessed=10**7, transcendentals=0),
+        name="own_mix",
+    )(head, in_hbm(part_own), in_hbm(part_far), side, rise, own)
     across, out = lax.optimization_barrier((across, out))
-    return mix(False, part_far, across, out)
+    return pl.pallas_call(
+        far_mix_kernel,
+        in_specs=[VMEM] * 4 + [HBM],
+        out_specs=HBM,
+        out_shape=out_type,
+        scratch_shapes=[held, tiles_16, tile_sems],
+        input_output_aliases={4: 0},
+        compiler_params=params(16),
+        name="far_mix",
+    )(part_far, side, rise, across, out)
 
 
 def solution(mesh):

time: 81.4 us -> 77 us (0.946)
  Pallas kernels: 44.9 us -> 39.4 us
  waiting for transfers between devices: 7.59 us -> 9.06 us
  starting transfers between devices: 25.5 us -> 24.4 us
    pallas_call x6, Pallas kernels: 32.6 us -> 27.3 us  [the longest x1 8.44 us: body(): pl.pallas_call(own_local_kernel, in_specs=[HBM] + [VMEM] * 5 + [HBM], out...]
    all_to_all x1, waiting for transfers between devices: 3.56 us -> 5.32 us  [body(): lax.all_to_all(joined, ALL, 0, 0, axis_index_groups=groups, tiled=True)]
    all_to_all x1, starting transfers between devices: 6.24 us -> 4.65 us  [body(): lax.all_to_all(prefixes, ALL, 0, 0, axis_index_groups=groups, tiled=True)]
  transfers between devices with their start and end apart: 6 -> 6, of which waited for: 2 -> 2; matrix products, arithmetic and copies ran while one was open for 1% -> 1% of each run, Pallas kernels for 41% -> 39%
where the time goes in v3:
time: 77 us; the launch traced here: 76.5 us
  Pallas kernels  39.4 us (51%)
  starting transfers between devices  24.4 us (32%)
  waiting for transfers between devices  9.06 us (12%)
  local copies, waits for them, and re-layouts  3.22 us (4%)
    all_to_all x1, starting transfers between devices, body(): lax.all_to_all(joined, ALL, 0, 0, axis_index_groups=groups, tiled=True)  10.8 us
    pallas_call x1, Pallas kernels, body(): pl.pallas_call(own_local_kernel, in_specs=[HBM] + [VMEM] * 5 + [HBM], out...  8.44 us
    pallas_call x1, Pallas kernels, body(): pl.pallas_call(far_local_kernel, in_specs=[HBM] * 2 + [VMEM] * 4 + [HBM],...  7.97 us
    pallas_call x1, Pallas kernels, body(): pl.pallas_call(lambda *refs: state_kernel(True, *refs), in_specs=[VMEM] *...  5.36 us
    all_to_all x1, waiting for transfers between devices, body(): lax.all_to_all(joined, ALL, 0, 0, axis_index_groups=groups, tiled=True)  5.32 us
    pallas_call x1, Pallas kernels, body(): pl.pallas_call(far_state_kernel, in_specs=[VMEM] * 6, out_specs=[HBM, VME...  5.3 us
    all_to_all x1, starting transfers between devices, body(): lax.all_to_all(prefixes, ALL, 0, 0, axis_index_groups=groups, tiled=True)  4.65 us
    ppermute x1, starting transfers between devices, body(): lax.ppermute(xbc[TOK - 8:], ALL, [(i, i + 1) for i in range(count - 1)])  4.5 us
  transfers between devices with their start and end apart: 6, of which 2 were waited for; matrix products, arithmetic and copies ran while one was open for 1% of the time, Pallas kernels for 39%

profile of v3, /device:TPU:1, one launch (start us, length us, event | category | flops | bytes accessed | tf_op | source)
XLA Modules:
  0.0 76.5 jit_solution(16198491966533838657)
XLA Ops:
  0.0 0.9 %slice.3 = bf16[8,5376]{1,0:T(8,128)(2,1)S(1)} slice(bf16[512,5376]{1,0:T(8,128)(2,1)} %x_hbm.1), slice={[504:512], [0:5376]} | slice | bytes 172032 | tf_op jit(solution)/shard_map/slice | solution.py:515
  0.9 4.5 %collective-permute-start = (bf16[8,5376]{1,0:T(8,128)(2,1)S(1)}, bf16[8,5376]{1,0:T(8,128)(2,1)S(1)}, u32[]{:S(2)}, u32[]{:S(2)}) collective-permute-start(bf16[8,5376]{1,0:T(8,128)(2,1)S(1)} %slice.3), channel_id=1, source_target_pairs={{0,1},{1,2},{2,3},{3,4},{4,5},{5,6},{6,7},{7,8},{8,9},{9,10},{10,1... | collective-permute-start | bytes 258056 | tf_op jit(solution)/shard_map/ppermute | solution.py:515
  5.4 0.8 broadcast_in_dim.7.bias_ref.refs_3_
  6.2 0.0 copy-start.1
  6.2 0.6 copy-done.1
  6.8 0.0 copy-start
  6.8 3.6 %fetch.1 = (bf16[512,5376]{1,0:T(8,128)(2,1)S(1)}, bf16[512,256]{1,0:T(8,128)(2,1)S(1)}, f32[8,128]{1,0:T(8,128)S(1)}, bf16[512,512]{1,0:T(8,128)(2,1)S(1)}, bf1...) custom-call(bf16[512,5376]{1,0:T(8,128)(2,1)} %x_hbm.1, f32[80,512]{1,0:T(8,128)} %dt_ref.1, f32[80,512]{1,0:T(8,128)} %log_ref.1, ...), custom_call_target="tpu_custom_call" | custom-call | tf_op jit(solution)/shard_map/fetch/pallas_call | solution.py:516
  10.4 0.0 collective-permute-done.rim_ref.refs_1_
  10.4 0.0 copy-done
  10.4 5.3 %far_states.1 = (bf16[5,512,512]{2,1,0:T(8,128)(2,1)}, bf16[64,48,128]{2,1,0:T(8,128)(2,1)S(1)}, bf16[512,256]{1,0:T(8,128)(2,1)S(1)}, bf16[128,512]{1,0:T(8,128)(2,1)S(1)}) custom-call(bf16[512,5376]{1,0:T(8,128)(2,1)S(1)} %get-tuple-element.42.x_ref.refs_0_, bf16[8,5376]{1,0:T(8,128)(2,1)S(1)} %collective-permute-done.rim_ref.refs_1_, ...), custom_call_target="tpu_custom_call" | custom-call | tf_op jit(solution)/shard_map/far_states/pallas_call | solution.py:541
  15.8 0.1 collective-permute-start.1
  15.8 5.4 %own_states.1 = (bf16[5,512,512]{2,1,0:T(8,128)(2,1)}, bf16[64,48,128]{2,1,0:T(8,128)(2,1)S(1)}, bf16[64,48,128]{2,1,0:T(8,128)(2,1)}) custom-call(bf16[512,5376]{1,0:T(8,128)(2,1)S(1)} %get-tuple-element.42.x_ref.refs_0_, bf16[8,5376]{1,0:T(8,128)(2,1)S(1)} %collective-permute-done.rim_ref.refs_1_, f32[4,5376]{1,0:T(4,128)S(1)} %copy-done, ...), custom_call_target="tpu_custom_call" | custom-call | flops 2000000000 | bytes 10000000 | tf_op jit(solution)/shard_map/own_states/pallas_call | solution.py:552
  21.2 0.0 collective-permute-done.1.got_ref
  21.2 1.2 %join_cores.1 = (bf16[64,48,128]{2,1,0:T(8,128)(2,1)}, bf16[64,48,128]{2,1,0:T(8,128)(2,1)}) custom-call(bf16[64,48,128]{2,1,0:T(8,128)(2,1)S(1)} %get-tuple-element.45.mine_ref, bf16[64,48,128]{2,1,0:T(8,128)(2,1)S(1)} %collective-permute-done.1.got_ref), custom_call_target="tpu_custom_call" | custom-call | tf_op jit(solution)/shard_map/join_cores/pallas_call | solution.py:563
  22.4 10.8 %all-to-all-start = ((bf16[64,48,128]{2,1,0:T(8,128)(2,1)}), bf16[64,48,128]{2,1,0:T(8,128)(2,1)S(1)}, u32[]{:S(2)}, u32[]{:S(2)}) async-start(bf16[64,48,128]{2,1,0:T(8,128)(2,1)} %get-tuple-element.47), calls=%async_computation | async-start | bytes 1572864 | tf_op jit(solution)/shard_map/all_to_all | solution.py:575
  33.3 1.3 %collective-permute-start.2 = (bf16[64,48,128]{2,1,0:T(8,128)(2,1)}, bf16[64,48,128]{2,1,0:T(8,128)(2,1)S(1)}, u32[]{:S(2)}, u32[]{:S(2)}) collective-permute-start(bf16[64,48,128]{2,1,0:T(8,128)(2,1)} %get-tuple-element.61), channel_id=1, source_target_pairs={{0,1},{2,3},{4,5},{6,7},{8,9},{10,11},{12,13},{14,15},{16,17},{18,... | collective-permute-start | bytes 2359304 | tf_op jit(solution)/shard_map/ppermute | solution.py:615
  34.6 8.4 %own_part.1 = (bf16[5,512,512]{2,1,0:T(8,128)(2,1)}, bf16[512,256]{1,0:T(8,128)(2,1)S(1)}, bf16[512,256]{1,0:T(8,128)(2,1)S(1)}) custom-call(bf16[5,512,512]{2,1,0:T(8,128)(2,1)} %get-tuple-element.48.values_hbm, bf16[512,256]{1,0:T(8,128)(2,1)S(1)} %get-tuple-element.50.side_ref, f32[512,128]{1,0:T(8,128)S(1)} %get-tuple-element.51.level_ref, ...), custom_call_target="tpu_custom_call" | custom-call | flops 1000000 | bytes 100000 | tf_op jit(solution)/shard_map/own_part/pallas_call | solution.py:588
  43.1 5.3 %all-to-all-done.refs_0_ = bf16[64,48,128]{2,1,0:T(8,128)(2,1)S(1)} async-done(((bf16[64,48,128]{2,1,0:T(8,128)(2,1)}), bf16[64,48,128]{2,1,0:T(8,128)(2,1)S(1)}, u32[]{:S(2)}, u32[]{:S(2)}) %all-to-all-start) | async-done | bytes 786464 | tf_op jit(solution)/shard_map/all_to_all | solution.py:575
  48.4 1.5 %scan_chips.1 = bf16[64,40,128]{2,1,0:T(8,128)(2,1)} custom-call(bf16[64,48,128]{2,1,0:T(8,128)(2,1)S(1)} %all-to-all-done.refs_0_), custom_call_target="tpu_custom_call" | custom-call | tf_op jit(solution)/shard_map/scan_chips/pallas_call | solution.py:599
  49.9 4.6 %all-to-all-start.1 = ((bf16[64,40,128]{2,1,0:T(8,128)(2,1)}), bf16[64,40,128]{2,1,0:T(8,128)(2,1)S(1)}, u32[]{:S(2)}, u32[]{:S(2)}) async-start(bf16[64,40,128]{2,1,0:T(8,128)(2,1)} %scan_chips.1), calls=%async_computation.1 | async-start | bytes 1310720 | tf_op jit(solution)/shard_map/all_to_all | solution.py:612
  54.5 0.0 collective-permute-done.2.start_hbm
  54.5 0.0 copy-start.2
  54.5 0.9 %copy-done.2 = bf16[64,48,128]{2,1,0:T(8,128)(2,1)} copy-done((bf16[64,48,128]{2,1,0:T(8,128)(2,1)}, bf16[64,48,128]{2,1,0:T(8,128)(2,1)S(1)}, u32[]{:S(2)}) %copy-start.2) | copy-done | bytes 786456
  55.5 8.0 %far_part.1 = (bf16[5,512,512]{2,1,0:T(8,128)(2,1)}, bf16[2,512,512]{2,1,0:T(8,128)(2,1)S(1)}) custom-call(bf16[5,512,512]{2,1,0:T(8,128)(2,1)} %get-tuple-element.58.values_hbm, bf16[5,512,512]{2,1,0:T(8,128)(2,1)} %get-tuple-element.59.part_own_hbm.part_hbm, bf16[512,256]{1,0:T(8,128)(2,1)S(1)} %get-tuple-element.60.both_ref, ...), custom_call_target="tpu_custom_call" | custom-call | flops 1000000 | bytes 100000 | tf_op jit(solution)/shard_map/far_part/pallas_call | solution.py:616
  63.4 3.7 %all-to-all-done.1.start_ref = bf16[64,40,128]{2,1,0:T(8,128)(2,1)S(1)} async-done(((bf16[64,40,128]{2,1,0:T(8,128)(2,1)}), bf16[64,40,128]{2,1,0:T(8,128)(2,1)S(1)}, u32[]{:S(2)}, u32[]{:S(2)}) %all-to-all-start.1) | async-done | bytes 655392 | tf_op jit(solution)/shard_map/all_to_all | solution.py:612
  67.2 3.1 %collective-permute-start.3 = (bf16[64,40,128]{2,1,0:T(8,128)(2,1)S(1)}, bf16[64,40,128]{2,1,0:T(8,128)(2,1)S(1)}, u32[]{:S(2)}, u32[]{:S(2)}) collective-permute-start(bf16[64,40,128]{2,1,0:T(8,128)(2,1)S(1)} %all-to-all-done.1.start_ref), channel_id=1, source_target_pairs={{0,1},{1,0},{2,3},{3,2},{4,5},{5,4},{6,7},{7,6},{8,9},{9,8},{10,11... | collective-permute-start | bytes 1966088 | tf_op jit(solution)/shard_map/ppermute | solution.py:627
  70.2 3.3 %own_mix.1 = (bf16[512,5120]{1,0:T(8,128)(2,1)}, bf16[5,512,512]{2,1,0:T(8,128)(2,1)S(1)}) custom-call(bf16[2,512,512]{2,1,0:T(8,128)(2,1)S(1)} %get-tuple-element.62.head_ref, bf16[5,512,512]{2,1,0:T(8,128)(2,1)} %get-tuple-element.59.part_own_hbm.part_hbm, bf16[5,512,512]{2,1,0:T(8,128)(2,1)} %get-tuple-element.64.far_part_hbm, ...), custom_call_target="tpu_custom_call" | custom-call | flops 1000000000 | bytes 10000000 | tf_op jit(solution)/shard_map/own_mix/pallas_call | solution.py:630
  73.5 0.0 collective-permute-done.3.start_ref
  73.5 2.8 %far_mix.1 = bf16[512,5120]{1,0:T(8,128)(2,1)} custom-call(bf16[5,512,512]{2,1,0:T(8,128)(2,1)S(1)} %get-tuple-element.67.part_ref, bf16[512,256]{1,0:T(8,128)(2,1)S(1)} %get-tuple-element.50.side_ref, bf16[512,256]{1,0:T(8,128)(2,1)S(1)} %get-tuple-element.65.rise_ref, ...), custom_call_target="tpu_custom_call", output_to_operand_aliasing={{}: (4, {})} | custom-call | tf_op jit(solution)/shard_map/far_mix/pallas_call | solution.py:643
Async XLA Ops:
  0.9 9.5 %collective-permute-start = (bf16[8,5376]{1,0:T(8,128)(2,1)S(1)}, bf16[8,5376]{1,0:T(8,128)(2,1)S(1)}, u32[]{:S(2)}, u32[]{:S(2)}) collective-permute-start(bf16[8,5376]{1,0:T(8,128)(2,1)S(1)} %slice.3), channel_id=1, source_target_pairs={{0,1},{1,2},{2,3},{3,4},{4,5},{5,6},{6,7},{7,8},{8,9},{9,10},{10,1... | collective-permute-start | bytes 258056 | tf_op jit(solution)/shard_map/ppermute | solution.py:515
  6.2 0.7 copy-start.1
  6.8 3.6 %copy-start = (f32[4,5376]{1,0:T(4,128)S(1)}, f32[4,5376]{1,0:T(4,128)}, u32[]{:S(2)}) copy-start(f32[4,5376]{1,0:T(4,128)} %refs_2_.1) | copy-start | bytes 258052
  15.8 5.5 %collective-permute-start.1 = (bf16[64,48,128]{2,1,0:T(8,128)(2,1)S(1)}, bf16[64,48,128]{2,1,0:T(8,128)(2,1)S(1)}, u32[]{:S(2)}, u32[]{:S(2)}) collective-permute-start(bf16[64,48,128]{2,1,0:T(8,128)(2,1)S(1)} %get-tuple-element.41), channel_id=1, source_target_pairs={{0,1},{1,0},{2,3},{3,2},{4,5},{5,4},{6,7},{7,6},{8,9},{9,8},{10,11... | collective-permute-start | bytes 2359304 | tf_op jit(solution)/shard_map/ppermute | solution.py:550
  22.4 25.9 %all-to-all-start = ((bf16[64,48,128]{2,1,0:T(8,128)(2,1)}), bf16[64,48,128]{2,1,0:T(8,128)(2,1)S(1)}, u32[]{:S(2)}, u32[]{:S(2)}) async-start(bf16[64,48,128]{2,1,0:T(8,128)(2,1)} %get-tuple-element.47), calls=%async_computation | async-start | bytes 1572864 | tf_op jit(solution)/shard_map/all_to_all | solution.py:575
  33.3 21.2 %collective-permute-start.2 = (bf16[64,48,128]{2,1,0:T(8,128)(2,1)}, bf16[64,48,128]{2,1,0:T(8,128)(2,1)S(1)}, u32[]{:S(2)}, u32[]{:S(2)}) collective-permute-start(bf16[64,48,128]{2,1,0:T(8,128)(2,1)} %get-tuple-element.61), channel_id=1, source_target_pairs={{0,1},{2,3},{4,5},{6,7},{8,9},{10,11},{12,13},{14,15},{16,17},{18,... | collective-permute-start | bytes 2359304 | tf_op jit(solution)/shard_map/ppermute | solution.py:615
  49.9 17.3 %all-to-all-start.1 = ((bf16[64,40,128]{2,1,0:T(8,128)(2,1)}), bf16[64,40,128]{2,1,0:T(8,128)(2,1)S(1)}, u32[]{:S(2)}, u32[]{:S(2)}) async-start(bf16[64,40,128]{2,1,0:T(8,128)(2,1)} %scan_chips.1), calls=%async_computation.1 | async-start | bytes 1310720 | tf_op jit(solution)/shard_map/all_to_all | solution.py:612
  54.5 0.9 %copy-start.2 = (bf16[64,48,128]{2,1,0:T(8,128)(2,1)}, bf16[64,48,128]{2,1,0:T(8,128)(2,1)S(1)}, u32[]{:S(2)}) copy-start(bf16[64,48,128]{2,1,0:T(8,128)(2,1)S(1)} %collective-permute-done.2.start_hbm) | copy-start | bytes 2359300
  67.2 6.4 %collective-permute-start.3 = (bf16[64,40,128]{2,1,0:T(8,128)(2,1)S(1)}, bf16[64,40,128]{2,1,0:T(8,128)(2,1)S(1)}, u32[]{:S(2)}, u32[]{:S(2)}) collective-permute-start(bf16[64,40,128]{2,1,0:T(8,128)(2,1)S(1)} %all-to-all-done.1.start_ref), channel_id=1, source_target_pairs={{0,1},{1,0},{2,3},{3,2},{4,5},{5,4},{6,7},{7,6},{8,9},{9,8},{10,11... | collective-permute-start | bytes 1966088 | tf_op jit(solution)/shard_map/ppermute | solution.py:627

commit v4 on v3

--- a/solution.py
+++ b/solution.py
@@ -85,12 +85,24 @@
     return jnp.concatenate([high, middle, low, jnp.zeros((5, LANES), F32)], axis=0)
 
 
+def half_lanes(half):
+    return pl.ds(pl.multiple_of(half * (INNER // 2), LANES), INNER // 2)
+
+
 def fetch_kernel(
-    x_hbm, dt_ref, log_ref, skip_ref,
-    x_ref, to_end_ref, tail_ref, factors_ref, halves_ref, level_ref, sem,
-):
-    copy = pltpu.make_async_copy(x_hbm, x_ref, sem)
-    copy.start()
+    x_hbm, weight_hbm, bias_ref, dt_ref, log_ref, skip_ref,
+    x_ref, x_side_ref, weight_ref, bias_row_ref,
+    to_end_ref, tail_ref, factors_ref, halves_ref, level_ref, sems,
+):
+    copies = [
+        pltpu.make_async_copy(weight_hbm, weight_ref, sems.at[0]),
+        pltpu.make_async_copy(x_hbm.at[:, INNER:WIDTH], x_side_ref, sems.at[1]),
+        pltpu.make_async_copy(x_hbm.at[:, half_lanes(half_of(False))], x_ref, sems.at[2]),
+    ]
+    for copy in copies:
+        copy.start()
+    for lane in range(0, WIDTH, LANES):
+        bias_row_ref[:, lane : lane + LANES] = bias_ref[lane : lane + LANES][None, :]
     decays = [running_decay(log_ref, dt_ref, q) for q in range(CHUNKS)]
     totals = [cumulative[CHUNK - 1 :, :] for cumulative, _ in decays]
     after = jnp.zeros((1, HEADS), F32)
@@ -115,14 +127,16 @@
             jnp.broadcast_to(pad_heads(jnp.exp(middle)), (8, LANES))
         )
     halves_ref[8 * CHUNKS :, :] = split_pair(jnp.broadcast_to(pad_heads(skip_ref[...]), (8, LANES)))
-    copy.wait()
-
-
-def conv_lanes(x_ref, rim_ref, weight_ref, bias_ref, span_ref, lane, after):
+    for copy in copies:
+        copy.wait()
+
+
+def conv_lanes(x_ref, rim_ref, weight_ref, bias_ref, span_ref, x_lane, lane, after):
+    x_lanes = pl.ds(x_lane, LANES)
     lanes = pl.ds(lane, LANES)
     span_ref[0:8, :] = rim_ref[:, lanes].astype(F32)
     for row in range(0, TOK, PIECE):
-        span_ref[8 + row : 8 + row + PIECE, :] = x_ref[row : row + PIECE, lanes].astype(F32)
+        span_ref[8 + row : 8 + row + PIECE, :] = x_ref[row : row + PIECE, x_lanes].astype(F32)
     taps = [0.5 * weight_ref[k : k + 1, lanes] for k in range(CONV)]
     start = 0.5 * bias_ref[:, lanes]
     for row in range(0, TOK, PIECE):
@@ -143,7 +157,8 @@
             side_ref[row : row + PIECE, g * LANES : (g + 1) * LANES] = values
 
         conv_lanes(
-            x_ref, rim_ref, weight_ref, bias_ref, span_ref.at[g], INNER + g * LANES, keep
+            x_ref, rim_ref, weight_ref, bias_ref, span_ref.at[g], g * LANES,
+            INNER + g * LANES, keep,
         )
     inputs_ref[...] = side_ref[:, 0:N_STATE].astype(F32).T.astype(BF16)
 
@@ -164,6 +179,7 @@
     def load(t, slot):
         scale_ref[slot] = dot(to_end_ref[...], spread(half * HALF_TILES + t))
         for g in range(GROUPS):
+            x_lane = pl.multiple_of(t * TILE + g * LANES, LANES)
             lane = pl.multiple_of(half * (INNER // 2) + t * TILE + g * LANES, LANES)
             local = slice(g * LANES, (g + 1) * LANES)
 
@@ -175,7 +191,8 @@
                 ).astype(BF16)
 
             conv_lanes(
-                x_ref, rim_ref, weight_ref, bias_ref, span_ref.at[slot * GROUPS + g], lane, keep
+                x_ref, rim_ref, weight_ref, bias_ref, span_ref.at[slot * GROUPS + g],
+                x_lane, lane, keep,
             )
         values_copy(t).start()
 
@@ -216,14 +233,17 @@
 
 
 def far_state_kernel(
-    x_ref, rim_ref, weight_ref, bias_ref, to_end_ref, tail_ref,
-    values_hbm, state_ref, side_ref, inputs_ref, span_ref, *scratch,
-):
-    side_values(x_ref, rim_ref, weight_ref, bias_ref, span_ref, side_ref, inputs_ref)
+    x_ref, x_side_ref, x_hbm, rim_ref, weight_ref, bias_ref, to_end_ref, tail_ref,
+    values_hbm, state_ref, side_ref, inputs_ref, x_own_ref, span_ref, *scratch,
+):
+    copy = pltpu.make_async_copy(x_hbm.at[:, half_lanes(half_of(True))], x_own_ref, scratch[-1])
+    copy.start()
+    side_values(x_side_ref, rim_ref, weight_ref, bias_ref, span_ref, side_ref, inputs_ref)
     state_kernel(
         False, x_ref, rim_ref, weight_ref, bias_ref, to_end_ref, tail_ref, inputs_ref,
-        values_hbm, state_ref, span_ref, *scratch,
-    )
+        values_hbm, state_ref, span_ref, *scratch[:-1],
+    )
+    copy.wait()
 
 
 def rows_of_heads(count, core):
@@ -513,23 +533,29 @@
     pair_out = jax.ShapeDtypeStruct((TOK, 2 * LANES), BF16)
 
     rim = lax.ppermute(xbc[TOK - 8 :], ALL, [(i, i + 1) for i in range(count - 1)])
-    x_near, to_end, tail, factors, halves, level = pl.pallas_call(
+    x_half = pltpu.VMEM((TOK, INNER // 2), BF16)
+    x_far, x_side, weight, bias, to_end, tail, factors, halves, level = pl.pallas_call(
         fetch_kernel,
-        in_specs=[HBM, VMEM, VMEM, VMEM],
-        out_specs=[VMEM] * 6,
+        in_specs=[HBM, HBM] + [VMEM] * 4,
+        out_specs=[VMEM] * 9,
         out_shape=[
-            pltpu.VMEM((TOK, WIDTH), BF16),
+            x_half,
+            pltpu.VMEM((TOK, 2 * N_STATE), BF16),
+            pltpu.VMEM((CONV, WIDTH), F32),
+            pltpu.VMEM((1, WIDTH), F32),
             pair_out,
             pltpu.VMEM((8, LANES), F32),
             jax.ShapeDtypeStruct((TOK, 4 * LANES), BF16),
             jax.ShapeDtypeStruct((8 * CHUNKS + 8, 2 * LANES), BF16),
             jax.ShapeDtypeStruct((TOK, LANES), F32),
         ],
-        scratch_shapes=[pltpu.SemaphoreType.DMA],
+        scratch_shapes=[pltpu.SemaphoreType.DMA((3,))],
         compiler_params=params(8),
         name="fetch",
-    )(in_hbm(xbc), in_hbm(dt), in_hbm(decay_log), skip[None, :])
-    bias = conv_bias[None, :]
+    )(
+        in_hbm(xbc), in_hbm(conv_weight), in_hbm(conv_bias), in_hbm(dt), in_hbm(decay_log),
+        in_hbm(skip[None, :]),
+    )
     state_scratch = [
         pltpu.VMEM((2 * GROUPS, 8 + TOK, LANES), F32),
         held,
@@ -538,17 +564,17 @@
         tiles_16,
         pltpu.SemaphoreType.DMA((HALF_TILES + 1,)),
     ]
-    values_far, other, side, inputs = pl.pallas_call(
+    values_far, other, side, inputs, x_own = pl.pallas_call(
         far_state_kernel,
-        in_specs=[VMEM] * 6,
-        out_specs=[HBM, VMEM, VMEM, VMEM],
-        out_shape=[half_out, state_out, pair_out, inputs_out],
-        scratch_shapes=state_scratch,
+        in_specs=[VMEM, VMEM, HBM] + [VMEM] * 5,
+        out_specs=[HBM] + [VMEM] * 4,
+        out_shape=[half_out, state_out, pair_out, inputs_out, x_half],
+        scratch_shapes=state_scratch + [pltpu.SemaphoreType.DMA],
         compiler_params=params(16),
         name="far_states",
-    )(x_near, rim, conv_weight, bias, to_end, tail)
+    )(x_far, x_side, in_hbm(xbc), rim, weight, bias, to_end, tail)
     got = lax.ppermute(other, "narrow", swap)
-    x_near, other = lax.optimization_barrier((x_near, other))
+    x_own, other = lax.optimization_barrier((x_own, other))
     values_own, mine, spare = pl.pallas_call(
         lambda *refs: state_kernel(True, *refs),
         in_specs=[VMEM] * 7,
@@ -558,7 +584,7 @@
         compiler_params=params(16),
         cost_estimate=pl.CostEstimate(flops=2 * 10**9, bytes_accessed=10**7, transcendentals=0),
         name="own_states",
-    )(x_near, rim, conv_weight, bias, to_end, tail, inputs)
+    )(x_own, rim, weight, bias, to_end, tail, inputs)
     got, mine = lax.optimization_barrier((got, mine))
     joined, got = pl.pallas_call(
         join_kernel,

time: 77 us -> 75 us (0.974)
  local copies, waits for them, and re-layouts: 3.22 us -> 1.83 us
    unnamed x6 -> x2, local copies, waits for them, and re-layouts: 1.57 us -> 0.93 us
  transfers between devices with their start and end apart: 6 -> 6, of which waited for: 2 -> 2; matrix products, arithmetic and copies ran while one was open for 1% -> 0% of each run, Pallas kernels for 39% -> 40%
where the time goes in v4:
time: 75 us; the launch traced here: 74.6 us
  Pallas kernels  38.7 us (52%)
  starting transfers between devices  24.4 us (33%)
  waiting for transfers between devices  9.29 us (12%)
  local copies, waits for them, and re-layouts  1.83 us (2%)
    all_to_all x1, starting transfers between devices, body(): lax.all_to_all(joined, ALL, 0, 0, axis_index_groups=groups, tiled=True)  10.9 us
    pallas_call x1, Pallas kernels, body(): pl.pallas_call(own_local_kernel, in_specs=[HBM] + [VMEM] * 5 + [HBM], out...  8.4 us
    pallas_call x1, Pallas kernels, body(): pl.pallas_call(far_local_kernel, in_specs=[HBM] * 2 + [VMEM] * 4 + [HBM],...  7.96 us
    all_to_all x1, waiting for transfers between devices, body(): lax.all_to_all(joined, ALL, 0, 0, axis_index_groups=groups, tiled=True)  5.45 us
    pallas_call x1, Pallas kernels, body(): pl.pallas_call(lambda *refs: state_kernel(True, *refs), in_specs=[VMEM] *...  5.39 us
    pallas_call x1, Pallas kernels, body(): pl.pallas_call(far_state_kernel, in_specs=[VMEM, VMEM, HBM] + [VMEM] * 5,...  5.3 us
    all_to_all x1, starting transfers between devices, body(): lax.all_to_all(prefixes, ALL, 0, 0, axis_index_groups=groups, tiled=True)  4.65 us
    ppermute x1, starting transfers between devices, body(): lax.ppermute(xbc[TOK - 8:], ALL, [(i, i + 1) for i in range(count - 1)])  4.5 us
  transfers between devices with their start and end apart: 6, of which 2 were waited for; matrix products, arithmetic and copies ran while one was open for 0% of the time, Pallas kernels for 40%

profile of v4, /device:TPU:1, one launch (start us, length us, event | category | flops | bytes accessed | tf_op | source)
XLA Modules:
  0.0 74.6 jit_solution(1031541106086382693)
XLA Ops:
  0.0 0.9 %slice.3 = bf16[8,5376]{1,0:T(8,128)(2,1)S(1)} slice(bf16[512,5376]{1,0:T(8,128)(2,1)} %x_hbm.3), slice={[504:512], [0:5376]} | slice | bytes 172032 | tf_op jit(solution)/shard_map/slice | solution.py:535
  0.9 4.5 %collective-permute-start = (bf16[8,5376]{1,0:T(8,128)(2,1)S(1)}, bf16[8,5376]{1,0:T(8,128)(2,1)S(1)}, u32[]{:S(2)}, u32[]{:S(2)}) collective-permute-start(bf16[8,5376]{1,0:T(8,128)(2,1)S(1)} %slice.3), channel_id=1, source_target_pairs={{0,1},{1,2},{2,3},{3,4},{4,5},{5,6},{6,7},{7,8},{8,9},{9,10},{10,1... | collective-permute-start | bytes 258056 | tf_op jit(solution)/shard_map/ppermute | solution.py:535
  5.4 3.0 %fetch.1 = (bf16[512,2560]{1,0:T(8,128)(2,1)S(1)}, bf16[512,256]{1,0:T(8,128)(2,1)S(1)}, f32[4,5376]{1,0:T(4,128)S(1)}, f32[1,5376]{1,0:T(1,128)S(1)}, bf16[512,...) custom-call(bf16[512,5376]{1,0:T(8,128)(2,1)} %x_hbm.3, ...), custom_call_target="tpu_custom_call" | custom-call | tf_op jit(solution)/shard_map/fetch/pallas_call | solution.py:537
  8.4 0.0 collective-permute-done.rim_ref.refs_1_
  8.4 5.3 %far_states.1 = (bf16[5,512,512]{2,1,0:T(8,128)(2,1)}, bf16[64,48,128]{2,1,0:T(8,128)(2,1)S(1)}, bf16[512,256]{1,0:T(8,128)(2,1)S(1)}, bf16[128,512]{1,0:T(8,128)(2,1)S(1)}, bf16[512,2560]{1,0:T(8,128)(2,1)S(1)}) custom-call(bf16[512,2560]{1,0:T(8,128)(2,1)S(1)} %get-tuple-element.42.x_ref, bf16[512,256]{1,0:T(8,128)(2,1)S(1)} %get-tuple-element.43.x_side_ref, ...), custom_call_target="tpu_custom_call" | custom-call | tf_op jit(solution)/shard_map/far_states/pallas_call | solution.py:567
  13.7 0.1 collective-permute-start.1
  13.8 5.4 %own_states.1 = (bf16[5,512,512]{2,1,0:T(8,128)(2,1)}, bf16[64,48,128]{2,1,0:T(8,128)(2,1)S(1)}, bf16[64,48,128]{2,1,0:T(8,128)(2,1)}) custom-call(bf16[512,2560]{1,0:T(8,128)(2,1)S(1)} %get-tuple-element.50.refs_0_, bf16[8,5376]{1,0:T(8,128)(2,1)S(1)} %collective-permute-done.rim_ref.refs_1_, f32[4,5376]{1,0:T(4,128)S(1)} %get-tuple-element.44.weight_ref.refs_2_, ...), custom_call_target="tpu_custom_call" | custom-call | flops 2000000000 | bytes 10000000 | tf_op jit(solution)/shard_map/own_states/pallas_call | solution.py:578
  19.2 0.0 collective-permute-done.1.got_ref
  19.2 1.2 %join_cores.1 = (bf16[64,48,128]{2,1,0:T(8,128)(2,1)}, bf16[64,48,128]{2,1,0:T(8,128)(2,1)}) custom-call(bf16[64,48,128]{2,1,0:T(8,128)(2,1)S(1)} %get-tuple-element.53.mine_ref, bf16[64,48,128]{2,1,0:T(8,128)(2,1)S(1)} %collective-permute-done.1.got_ref), custom_call_target="tpu_custom_call" | custom-call | tf_op jit(solution)/shard_map/join_cores/pallas_call | solution.py:589
  20.4 10.9 %all-to-all-start = ((bf16[64,48,128]{2,1,0:T(8,128)(2,1)}), bf16[64,48,128]{2,1,0:T(8,128)(2,1)S(1)}, u32[]{:S(2)}, u32[]{:S(2)}) async-start(bf16[64,48,128]{2,1,0:T(8,128)(2,1)} %get-tuple-element.55), calls=%async_computation | async-start | bytes 1572864 | tf_op jit(solution)/shard_map/all_to_all | solution.py:601
  31.3 1.3 %collective-permute-start.2 = (bf16[64,48,128]{2,1,0:T(8,128)(2,1)}, bf16[64,48,128]{2,1,0:T(8,128)(2,1)S(1)}, u32[]{:S(2)}, u32[]{:S(2)}) collective-permute-start(bf16[64,48,128]{2,1,0:T(8,128)(2,1)} %get-tuple-element.69), channel_id=1, source_target_pairs={{0,1},{2,3},{4,5},{6,7},{8,9},{10,11},{12,13},{14,15},{16,17},{18,... | collective-permute-start | bytes 2359304 | tf_op jit(solution)/shard_map/ppermute | solution.py:641
  32.6 8.4 %own_part.1 = (bf16[5,512,512]{2,1,0:T(8,128)(2,1)}, bf16[512,256]{1,0:T(8,128)(2,1)S(1)}, bf16[512,256]{1,0:T(8,128)(2,1)S(1)}) custom-call(bf16[5,512,512]{2,1,0:T(8,128)(2,1)} %get-tuple-element.56.values_hbm, bf16[512,256]{1,0:T(8,128)(2,1)S(1)} %get-tuple-element.58.side_ref, f32[512,128]{1,0:T(8,128)S(1)} %get-tuple-element.59.level_ref, ...), custom_call_target="tpu_custom_call" | custom-call | flops 1000000 | bytes 100000 | tf_op jit(solution)/shard_map/own_part/pallas_call | solution.py:614
  41.0 5.5 %all-to-all-done.refs_0_ = bf16[64,48,128]{2,1,0:T(8,128)(2,1)S(1)} async-done(((bf16[64,48,128]{2,1,0:T(8,128)(2,1)}), bf16[64,48,128]{2,1,0:T(8,128)(2,1)S(1)}, u32[]{:S(2)}, u32[]{:S(2)}) %all-to-all-start) | async-done | bytes 786464 | tf_op jit(solution)/shard_map/all_to_all | solution.py:601
  46.5 1.5 %scan_chips.1 = bf16[64,40,128]{2,1,0:T(8,128)(2,1)} custom-call(bf16[64,48,128]{2,1,0:T(8,128)(2,1)S(1)} %all-to-all-done.refs_0_), custom_call_target="tpu_custom_call" | custom-call | tf_op jit(solution)/shard_map/scan_chips/pallas_call | solution.py:625
  48.0 4.6 %all-to-all-start.1 = ((bf16[64,40,128]{2,1,0:T(8,128)(2,1)}), bf16[64,40,128]{2,1,0:T(8,128)(2,1)S(1)}, u32[]{:S(2)}, u32[]{:S(2)}) async-start(bf16[64,40,128]{2,1,0:T(8,128)(2,1)} %scan_chips.1), calls=%async_computation.1 | async-start | bytes 1310720 | tf_op jit(solution)/shard_map/all_to_all | solution.py:638
  52.6 0.0 collective-permute-done.2.start_hbm
  52.7 0.0 copy-start
  52.7 0.9 %copy-done = bf16[64,48,128]{2,1,0:T(8,128)(2,1)} copy-done((bf16[64,48,128]{2,1,0:T(8,128)(2,1)}, bf16[64,48,128]{2,1,0:T(8,128)(2,1)S(1)}, u32[]{:S(2)}) %copy-start) | copy-done | bytes 786456
  53.6 8.0 %far_part.1 = (bf16[5,512,512]{2,1,0:T(8,128)(2,1)}, bf16[2,512,512]{2,1,0:T(8,128)(2,1)S(1)}) custom-call(bf16[5,512,512]{2,1,0:T(8,128)(2,1)} %get-tuple-element.66.values_hbm, bf16[5,512,512]{2,1,0:T(8,128)(2,1)} %get-tuple-element.67.part_own_hbm.part_hbm, bf16[512,256]{1,0:T(8,128)(2,1)S(1)} %get-tuple-element.68.both_ref, ...), custom_call_target="tpu_custom_call" | custom-call | flops 1000000 | bytes 100000 | tf_op jit(solution)/shard_map/far_part/pallas_call | solution.py:642
  61.6 3.8 %all-to-all-done.1.start_ref = bf16[64,40,128]{2,1,0:T(8,128)(2,1)S(1)} async-done(((bf16[64,40,128]{2,1,0:T(8,128)(2,1)}), bf16[64,40,128]{2,1,0:T(8,128)(2,1)S(1)}, u32[]{:S(2)}, u32[]{:S(2)}) %all-to-all-start.1) | async-done | bytes 655392 | tf_op jit(solution)/shard_map/all_to_all | solution.py:638
  65.4 3.0 %collective-permute-start.3 = (bf16[64,40,128]{2,1,0:T(8,128)(2,1)S(1)}, bf16[64,40,128]{2,1,0:T(8,128)(2,1)S(1)}, u32[]{:S(2)}, u32[]{:S(2)}) collective-permute-start(bf16[64,40,128]{2,1,0:T(8,128)(2,1)S(1)} %all-to-all-done.1.start_ref), channel_id=1, source_target_pairs={{0,1},{1,0},{2,3},{3,2},{4,5},{5,4},{6,7},{7,6},{8,9},{9,8},{10,11... | collective-permute-start | bytes 1966088 | tf_op jit(solution)/shard_map/ppermute | solution.py:653
  68.3 3.3 %own_mix.1 = (bf16[512,5120]{1,0:T(8,128)(2,1)}, bf16[5,512,512]{2,1,0:T(8,128)(2,1)S(1)}) custom-call(bf16[2,512,512]{2,1,0:T(8,128)(2,1)S(1)} %get-tuple-element.70.head_ref, bf16[5,512,512]{2,1,0:T(8,128)(2,1)} %get-tuple-element.67.part_own_hbm.part_hbm, bf16[5,512,512]{2,1,0:T(8,128)(2,1)} %get-tuple-element.72.far_part_hbm, ...), custom_call_target="tpu_custom_call" | custom-call | flops 1000000000 | bytes 10000000 | tf_op jit(solution)/shard_map/own_mix/pallas_call | solution.py:656
  71.7 0.0 collective-permute-done.3.start_ref
  71.7 2.8 %far_mix.1 = bf16[512,5120]{1,0:T(8,128)(2,1)} custom-call(bf16[5,512,512]{2,1,0:T(8,128)(2,1)S(1)} %get-tuple-element.75.part_ref, bf16[512,256]{1,0:T(8,128)(2,1)S(1)} %get-tuple-element.58.side_ref, bf16[512,256]{1,0:T(8,128)(2,1)S(1)} %get-tuple-element.73.rise_ref, ...), custom_call_target="tpu_custom_call", output_to_operand_aliasing={{}: (4, {})} | custom-call | tf_op jit(solution)/shard_map/far_mix/pallas_call | solution.py:669
Async XLA Ops:
  0.9 7.5 %collective-permute-start = (bf16[8,5376]{1,0:T(8,128)(2,1)S(1)}, bf16[8,5376]{1,0:T(8,128)(2,1)S(1)}, u32[]{:S(2)}, u32[]{:S(2)}) collective-permute-start(bf16[8,5376]{1,0:T(8,128)(2,1)S(1)} %slice.3), channel_id=1, source_target_pairs={{0,1},{1,2},{2,3},{3,4},{4,5},{5,6},{6,7},{7,8},{8,9},{9,10},{10,1... | collective-permute-start | bytes 258056 | tf_op jit(solution)/shard_map/ppermute | solution.py:535
  13.7 5.5 %collective-permute-start.1 = (bf16[64,48,128]{2,1,0:T(8,128)(2,1)S(1)}, bf16[64,48,128]{2,1,0:T(8,128)(2,1)S(1)}, u32[]{:S(2)}, u32[]{:S(2)}) collective-permute-start(bf16[64,48,128]{2,1,0:T(8,128)(2,1)S(1)} %get-tuple-element.48), channel_id=1, source_target_pairs={{0,1},{1,0},{2,3},{3,2},{4,5},{5,4},{6,7},{7,6},{8,9},{9,8},{10,11... | collective-permute-start | bytes 2359304 | tf_op jit(solution)/shard_map/ppermute | solution.py:576
  20.4 26.1 %all-to-all-start = ((bf16[64,48,128]{2,1,0:T(8,128)(2,1)}), bf16[64,48,128]{2,1,0:T(8,128)(2,1)S(1)}, u32[]{:S(2)}, u32[]{:S(2)}) async-start(bf16[64,48,128]{2,1,0:T(8,128)(2,1)} %get-tuple-element.55), calls=%async_computation | async-start | bytes 1572864 | tf_op jit(solution)/shard_map/all_to_all | solution.py:601
  31.3 21.3 %collective-permute-start.2 = (bf16[64,48,128]{2,1,0:T(8,128)(2,1)}, bf16[64,48,128]{2,1,0:T(8,128)(2,1)S(1)}, u32[]{:S(2)}, u32[]{:S(2)}) collective-permute-start(bf16[64,48,128]{2,1,0:T(8,128)(2,1)} %get-tuple-element.69), channel_id=1, source_target_pairs={{0,1},{2,3},{4,5},{6,7},{8,9},{10,11},{12,13},{14,15},{16,17},{18,... | collective-permute-start | bytes 2359304 | tf_op jit(solution)/shard_map/ppermute | solution.py:641
  48.0 17.4 %all-to-all-start.1 = ((bf16[64,40,128]{2,1,0:T(8,128)(2,1)}), bf16[64,40,128]{2,1,0:T(8,128)(2,1)S(1)}, u32[]{:S(2)}, u32[]{:S(2)}) async-start(bf16[64,40,128]{2,1,0:T(8,128)(2,1)} %scan_chips.1), calls=%async_computation.1 | async-start | bytes 1310720 | tf_op jit(solution)/shard_map/all_to_all | solution.py:638
  52.7 0.9 %copy-start = (bf16[64,48,128]{2,1,0:T(8,128)(2,1)}, bf16[64,48,128]{2,1,0:T(8,128)(2,1)S(1)}, u32[]{:S(2)}) copy-start(bf16[64,48,128]{2,1,0:T(8,128)(2,1)S(1)} %collective-permute-done.2.start_hbm) | copy-start | bytes 2359300
  65.4 6.3 %collective-permute-start.3 = (bf16[64,40,128]{2,1,0:T(8,128)(2,1)S(1)}, bf16[64,40,128]{2,1,0:T(8,128)(2,1)S(1)}, u32[]{:S(2)}, u32[]{:S(2)}) collective-permute-start(bf16[64,40,128]{2,1,0:T(8,128)(2,1)S(1)} %all-to-all-done.1.start_ref), channel_id=1, source_target_pairs={{0,1},{1,0},{2,3},{3,2},{4,5},{5,4},{6,7},{7,6},{8,9},{9,8},{10,11... | collective-permute-start | bytes 1966088 | tf_op jit(solution)/shard_map/ppermute | solution.py:653

commit v5 on v4

--- a/solution.py
+++ b/solution.py
@@ -7,6 +7,7 @@
 
 HEADS = 80
 HEAD_DIM = 64
+HEAD_SHIFT = 6
 N_STATE = 128
 CONV = 4
 INNER = 5120
@@ -59,8 +60,8 @@
 
 
 def spread(tile):
-    head = iota((2 * LANES, TILE), 0) % LANES
-    lane = iota((2 * LANES, TILE), 1) // HEAD_DIM
+    head = lax.bitwise_and(iota((2 * LANES, TILE), 0), LANES - 1)
+    lane = lax.shift_right_logical(iota((2 * LANES, TILE), 1), HEAD_SHIFT)
     return (head == lane + tile * (TILE // HEAD_DIM)).astype(F32).astype(BF16)
 
 
@@ -143,7 +144,7 @@
         half = start
         for k in range(CONV):
             half = half + span_ref[5 + k + row : 5 + k + row + PIECE, :] * taps[k]
-        after((half + half * jnp.tanh(half)).astype(BF16), row)
+        after(half + half * jnp.tanh(half), row)
 
 
 def half_of(own):
@@ -154,7 +155,7 @@
     for g in range(2):
 
         def keep(values, row, g=g):
-            side_ref[row : row + PIECE, g * LANES : (g + 1) * LANES] = values
+            side_ref[row : row + PIECE, g * LANES : (g + 1) * LANES] = values.astype(BF16)
 
         conv_lanes(
             x_ref, rim_ref, weight_ref, bias_ref, span_ref.at[g], g * LANES,
@@ -185,9 +186,9 @@
 
             def keep(values, row, local=local):
                 piece = slice(row, row + PIECE)
-                values_ref[t, piece, local] = values
+                values_ref[t, piece, local] = values.astype(BF16)
                 loaded_ref[slot, piece, local] = (
-                    values.astype(F32) * scale_ref[slot, piece, local]
+                    values * scale_ref[slot, piece, local]
                 ).astype(BF16)
 
             conv_lanes(
@@ -246,10 +247,11 @@
     copy.wait()
 
 
-def rows_of_heads(count, core):
-    row = lax.rem(iota((count, ROWS, LANES), 1), HALF_GROUPS)
-    head = iota((count, ROWS, LANES), 2)
-    return (head // 2 == row + core * HALF_GROUPS).astype(F32)
+def rows_of_heads(core):
+    row = iota((ROWS, LANES), 0)
+    row = jnp.where(row >= HALF_GROUPS, row - HALF_GROUPS, row)
+    pair = lax.shift_right_logical(iota((ROWS, LANES), 1), 1)
+    return (pair == row + core * HALF_GROUPS).astype(F32)[None]
 
 
 def lanes_of_heads():
@@ -258,7 +260,7 @@
 
 
 def decay_rows(high, middle, count, core):
-    mask = rows_of_heads(count, core)
+    mask = rows_of_heads(core)
     both = jnp.concatenate([mask * high, mask * middle], axis=2).astype(BF16)
     return dot(both.reshape(count * ROWS, 2 * LANES), lanes_of_heads())
 

time: 75 us -> 74.7 us (level)
  transfers between devices with their start and end apart: 6 -> 6, of which waited for: 2 -> 2; matrix products, arithmetic and copies ran while one was open for 0% -> 0% of each run, Pallas kernels for 40% -> 39%
where the time goes in v5:
time: 74.7 us; the launch traced here: 74.3 us
  Pallas kernels  38.1 us (51%)
  starting transfers between devices  24.6 us (33%)
  waiting for transfers between devices  9.47 us (13%)
  local copies, waits for them, and re-layouts  1.83 us (2%)
    all_to_all x1, starting transfers between devices, body(): lax.all_to_all(joined, ALL, 0, 0, axis_index_groups=groups, tiled=True)  10.9 us
    pallas_call x1, Pallas kernels, body(): pl.pallas_call(own_local_kernel, in_specs=[HBM] + [VMEM] * 5 + [HBM], out...  8.25 us
    pallas_call x1, Pallas kernels, body(): pl.pallas_call(far_local_kernel, in_specs=[HBM] * 2 + [VMEM] * 4 + [HBM],...  7.94 us
    all_to_all x1, waiting for transfers between devices, body(): lax.all_to_all(joined, ALL, 0, 0, axis_index_groups=groups, tiled=True)  5.61 us
    pallas_call x1, Pallas kernels, body(): pl.pallas_call(lambda *refs: state_kernel(True, *refs), in_specs=[VMEM] *...  5.12 us
    pallas_call x1, Pallas kernels, body(): pl.pallas_call(far_state_kernel, in_specs=[VMEM, VMEM, HBM] + [VMEM] * 5,...  5.1 us
    all_to_all x1, starting transfers between devices, body(): lax.all_to_all(prefixes, ALL, 0, 0, axis_index_groups=groups, tiled=True)  4.83 us
    ppermute x1, starting transfers between devices, body(): lax.ppermute(xbc[TOK - 8:], ALL, [(i, i + 1) for i in range(count - 1)])  4.5 us
  transfers between devices with their start and end apart: 6, of which 2 were waited for; matrix products, arithmetic and copies ran while one was open for 0% of the time, Pallas kernels for 39%

profile of v5, /device:TPU:1, one launch (start us, length us, event | category | flops | bytes accessed | tf_op | source)
XLA Modules:
  0.0 74.3 jit_solution(13547262572754360055)
XLA Ops:
  0.0 0.9 %slice.3 = bf16[8,5376]{1,0:T(8,128)(2,1)S(1)} slice(bf16[512,5376]{1,0:T(8,128)(2,1)} %x_hbm.3), slice={[504:512], [0:5376]} | slice | bytes 172032 | tf_op jit(solution)/shard_map/slice | solution.py:537
  0.9 4.5 %collective-permute-start = (bf16[8,5376]{1,0:T(8,128)(2,1)S(1)}, bf16[8,5376]{1,0:T(8,128)(2,1)S(1)}, u32[]{:S(2)}, u32[]{:S(2)}) collective-permute-start(bf16[8,5376]{1,0:T(8,128)(2,1)S(1)} %slice.3), channel_id=1, source_target_pairs={{0,1},{1,2},{2,3},{3,4},{4,5},{5,6},{6,7},{7,8},{8,9},{9,10},{10,1... | collective-permute-start | bytes 258056 | tf_op jit(solution)/shard_map/ppermute | solution.py:537
  5.4 3.0 %fetch.1 = (bf16[512,2560]{1,0:T(8,128)(2,1)S(1)}, bf16[512,256]{1,0:T(8,128)(2,1)S(1)}, f32[4,5376]{1,0:T(4,128)S(1)}, f32[1,5376]{1,0:T(1,128)S(1)}, bf16[512,...) custom-call(bf16[512,5376]{1,0:T(8,128)(2,1)} %x_hbm.3, ...), custom_call_target="tpu_custom_call" | custom-call | tf_op jit(solution)/shard_map/fetch/pallas_call | solution.py:539
  8.4 0.0 collective-permute-done.rim_ref.refs_1_
  8.4 5.1 %far_states.1 = (bf16[5,512,512]{2,1,0:T(8,128)(2,1)}, bf16[64,48,128]{2,1,0:T(8,128)(2,1)S(1)}, bf16[512,256]{1,0:T(8,128)(2,1)S(1)}, bf16[128,512]{1,0:T(8,128)(2,1)S(1)}, bf16[512,2560]{1,0:T(8,128)(2,1)S(1)}) custom-call(bf16[512,2560]{1,0:T(8,128)(2,1)S(1)} %get-tuple-element.42.x_ref, bf16[512,256]{1,0:T(8,128)(2,1)S(1)} %get-tuple-element.43.x_side_ref, ...), custom_call_target="tpu_custom_call" | custom-call | tf_op jit(solution)/shard_map/far_states/pallas_call | solution.py:569
  13.5 0.1 collective-permute-start.1
  13.6 5.1 %own_states.1 = (bf16[5,512,512]{2,1,0:T(8,128)(2,1)}, bf16[64,48,128]{2,1,0:T(8,128)(2,1)S(1)}, bf16[64,48,128]{2,1,0:T(8,128)(2,1)}) custom-call(bf16[512,2560]{1,0:T(8,128)(2,1)S(1)} %get-tuple-element.50.refs_0_, bf16[8,5376]{1,0:T(8,128)(2,1)S(1)} %collective-permute-done.rim_ref.refs_1_, f32[4,5376]{1,0:T(4,128)S(1)} %get-tuple-element.44.weight_ref.refs_2_, ...), custom_call_target="tpu_custom_call" | custom-call | flops 2000000000 | bytes 10000000 | tf_op jit(solution)/shard_map/own_states/pallas_call | solution.py:580
  18.7 0.0 collective-permute-done.1.got_ref
  18.7 1.2 %join_cores.1 = (bf16[64,48,128]{2,1,0:T(8,128)(2,1)}, bf16[64,48,128]{2,1,0:T(8,128)(2,1)}) custom-call(bf16[64,48,128]{2,1,0:T(8,128)(2,1)S(1)} %get-tuple-element.53.mine_ref, bf16[64,48,128]{2,1,0:T(8,128)(2,1)S(1)} %collective-permute-done.1.got_ref), custom_call_target="tpu_custom_call" | custom-call | tf_op jit(solution)/shard_map/join_cores/pallas_call | solution.py:591
  19.9 10.9 %all-to-all-start = ((bf16[64,48,128]{2,1,0:T(8,128)(2,1)}), bf16[64,48,128]{2,1,0:T(8,128)(2,1)S(1)}, u32[]{:S(2)}, u32[]{:S(2)}) async-start(bf16[64,48,128]{2,1,0:T(8,128)(2,1)} %get-tuple-element.55), calls=%async_computation | async-start | bytes 1572864 | tf_op jit(solution)/shard_map/all_to_all | solution.py:603
  30.9 1.3 %collective-permute-start.2 = (bf16[64,48,128]{2,1,0:T(8,128)(2,1)}, bf16[64,48,128]{2,1,0:T(8,128)(2,1)S(1)}, u32[]{:S(2)}, u32[]{:S(2)}) collective-permute-start(bf16[64,48,128]{2,1,0:T(8,128)(2,1)} %get-tuple-element.69), channel_id=1, source_target_pairs={{0,1},{2,3},{4,5},{6,7},{8,9},{10,11},{12,13},{14,15},{16,17},{18,... | collective-permute-start | bytes 2359304 | tf_op jit(solution)/shard_map/ppermute | solution.py:643
  32.2 8.2 %own_part.1 = (bf16[5,512,512]{2,1,0:T(8,128)(2,1)}, bf16[512,256]{1,0:T(8,128)(2,1)S(1)}, bf16[512,256]{1,0:T(8,128)(2,1)S(1)}) custom-call(bf16[5,512,512]{2,1,0:T(8,128)(2,1)} %get-tuple-element.56.values_hbm, bf16[512,256]{1,0:T(8,128)(2,1)S(1)} %get-tuple-element.58.side_ref, f32[512,128]{1,0:T(8,128)S(1)} %get-tuple-element.59.level_ref, ...), custom_call_target="tpu_custom_call" | custom-call | flops 1000000 | bytes 100000 | tf_op jit(solution)/shard_map/own_part/pallas_call | solution.py:616
  40.4 5.6 %all-to-all-done.refs_0_ = bf16[64,48,128]{2,1,0:T(8,128)(2,1)S(1)} async-done(((bf16[64,48,128]{2,1,0:T(8,128)(2,1)}), bf16[64,48,128]{2,1,0:T(8,128)(2,1)S(1)}, u32[]{:S(2)}, u32[]{:S(2)}) %all-to-all-start) | async-done | bytes 786464 | tf_op jit(solution)/shard_map/all_to_all | solution.py:603
  46.0 1.5 %scan_chips.1 = bf16[64,40,128]{2,1,0:T(8,128)(2,1)} custom-call(bf16[64,48,128]{2,1,0:T(8,128)(2,1)S(1)} %all-to-all-done.refs_0_), custom_call_target="tpu_custom_call" | custom-call | tf_op jit(solution)/shard_map/scan_chips/pallas_call | solution.py:627
  47.5 4.8 %all-to-all-start.1 = ((bf16[64,40,128]{2,1,0:T(8,128)(2,1)}), bf16[64,40,128]{2,1,0:T(8,128)(2,1)S(1)}, u32[]{:S(2)}, u32[]{:S(2)}) async-start(bf16[64,40,128]{2,1,0:T(8,128)(2,1)} %scan_chips.1), calls=%async_computation.1 | async-start | bytes 1310720 | tf_op jit(solution)/shard_map/all_to_all | solution.py:640
  52.4 0.0 collective-permute-done.2.start_hbm
  52.4 0.0 copy-start
  52.4 0.9 %copy-done = bf16[64,48,128]{2,1,0:T(8,128)(2,1)} copy-done((bf16[64,48,128]{2,1,0:T(8,128)(2,1)}, bf16[64,48,128]{2,1,0:T(8,128)(2,1)S(1)}, u32[]{:S(2)}) %copy-start) | copy-done | bytes 786456
  53.3 7.9 %far_part.1 = (bf16[5,512,512]{2,1,0:T(8,128)(2,1)}, bf16[2,512,512]{2,1,0:T(8,128)(2,1)S(1)}) custom-call(bf16[5,512,512]{2,1,0:T(8,128)(2,1)} %get-tuple-element.66.values_hbm, bf16[5,512,512]{2,1,0:T(8,128)(2,1)} %get-tuple-element.67.part_own_hbm.part_hbm, bf16[512,256]{1,0:T(8,128)(2,1)S(1)} %get-tuple-element.68.both_ref, ...), custom_call_target="tpu_custom_call" | custom-call | flops 1000000 | bytes 100000 | tf_op jit(solution)/shard_map/far_part/pallas_call | solution.py:644
  61.3 3.9 %all-to-all-done.1.start_ref = bf16[64,40,128]{2,1,0:T(8,128)(2,1)S(1)} async-done(((bf16[64,40,128]{2,1,0:T(8,128)(2,1)}), bf16[64,40,128]{2,1,0:T(8,128)(2,1)S(1)}, u32[]{:S(2)}, u32[]{:S(2)}) %all-to-all-start.1) | async-done | bytes 655392 | tf_op jit(solution)/shard_map/all_to_all | solution.py:640
  65.1 3.0 %collective-permute-start.3 = (bf16[64,40,128]{2,1,0:T(8,128)(2,1)S(1)}, bf16[64,40,128]{2,1,0:T(8,128)(2,1)S(1)}, u32[]{:S(2)}, u32[]{:S(2)}) collective-permute-start(bf16[64,40,128]{2,1,0:T(8,128)(2,1)S(1)} %all-to-all-done.1.start_ref), channel_id=1, source_target_pairs={{0,1},{1,0},{2,3},{3,2},{4,5},{5,4},{6,7},{7,6},{8,9},{9,8},{10,11... | collective-permute-start | bytes 1966088 | tf_op jit(solution)/shard_map/ppermute | solution.py:655
  68.1 3.3 %own_mix.1 = (bf16[512,5120]{1,0:T(8,128)(2,1)}, bf16[5,512,512]{2,1,0:T(8,128)(2,1)S(1)}) custom-call(bf16[2,512,512]{2,1,0:T(8,128)(2,1)S(1)} %get-tuple-element.70.head_ref, bf16[5,512,512]{2,1,0:T(8,128)(2,1)} %get-tuple-element.67.part_own_hbm.part_hbm, bf16[5,512,512]{2,1,0:T(8,128)(2,1)} %get-tuple-element.72.far_part_hbm, ...), custom_call_target="tpu_custom_call" | custom-call | flops 1000000000 | bytes 10000000 | tf_op jit(solution)/shard_map/own_mix/pallas_call | solution.py:658
  71.4 0.0 collective-permute-done.3.start_ref
  71.4 2.7 %far_mix.1 = bf16[512,5120]{1,0:T(8,128)(2,1)} custom-call(bf16[5,512,512]{2,1,0:T(8,128)(2,1)S(1)} %get-tuple-element.75.part_ref, bf16[512,256]{1,0:T(8,128)(2,1)S(1)} %get-tuple-element.58.side_ref, bf16[512,256]{1,0:T(8,128)(2,1)S(1)} %get-tuple-element.73.rise_ref, ...), custom_call_target="tpu_custom_call", output_to_operand_aliasing={{}: (4, {})} | custom-call | tf_op jit(solution)/shard_map/far_mix/pallas_call | solution.py:671
Async XLA Ops:
  0.9 7.5 %collective-permute-start = (bf16[8,5376]{1,0:T(8,128)(2,1)S(1)}, bf16[8,5376]{1,0:T(8,128)(2,1)S(1)}, u32[]{:S(2)}, u32[]{:S(2)}) collective-permute-start(bf16[8,5376]{1,0:T(8,128)(2,1)S(1)} %slice.3), channel_id=1, source_target_pairs={{0,1},{1,2},{2,3},{3,4},{4,5},{5,6},{6,7},{7,8},{8,9},{9,10},{10,1... | collective-permute-start | bytes 258056 | tf_op jit(solution)/shard_map/ppermute | solution.py:537
  13.5 5.2 %collective-permute-start.1 = (bf16[64,48,128]{2,1,0:T(8,128)(2,1)S(1)}, bf16[64,48,128]{2,1,0:T(8,128)(2,1)S(1)}, u32[]{:S(2)}, u32[]{:S(2)}) collective-permute-start(bf16[64,48,128]{2,1,0:T(8,128)(2,1)S(1)} %get-tuple-element.48), channel_id=1, source_target_pairs={{0,1},{1,0},{2,3},{3,2},{4,5},{5,4},{6,7},{7,6},{8,9},{9,8},{10,11... | collective-permute-start | bytes 2359304 | tf_op jit(solution)/shard_map/ppermute | solution.py:578
  19.9 26.1 %all-to-all-start = ((bf16[64,48,128]{2,1,0:T(8,128)(2,1)}), bf16[64,48,128]{2,1,0:T(8,128)(2,1)S(1)}, u32[]{:S(2)}, u32[]{:S(2)}) async-start(bf16[64,48,128]{2,1,0:T(8,128)(2,1)} %get-tuple-element.55), calls=%async_computation | async-start | bytes 1572864 | tf_op jit(solution)/shard_map/all_to_all | solution.py:603
  30.9 21.5 %collective-permute-start.2 = (bf16[64,48,128]{2,1,0:T(8,128)(2,1)}, bf16[64,48,128]{2,1,0:T(8,128)(2,1)S(1)}, u32[]{:S(2)}, u32[]{:S(2)}) collective-permute-start(bf16[64,48,128]{2,1,0:T(8,128)(2,1)} %get-tuple-element.69), channel_id=1, source_target_pairs={{0,1},{2,3},{4,5},{6,7},{8,9},{10,11},{12,13},{14,15},{16,17},{18,... | collective-permute-start | bytes 2359304 | tf_op jit(solution)/shard_map/ppermute | solution.py:643
  47.5 17.6 %all-to-all-start.1 = ((bf16[64,40,128]{2,1,0:T(8,128)(2,1)}), bf16[64,40,128]{2,1,0:T(8,128)(2,1)S(1)}, u32[]{:S(2)}, u32[]{:S(2)}) async-start(bf16[64,40,128]{2,1,0:T(8,128)(2,1)} %scan_chips.1), calls=%async_computation.1 | async-start | bytes 1310720 | tf_op jit(solution)/shard_map/all_to_all | solution.py:640
  52.4 0.9 %copy-start = (bf16[64,48,128]{2,1,0:T(8,128)(2,1)}, bf16[64,48,128]{2,1,0:T(8,128)(2,1)S(1)}, u32[]{:S(2)}) copy-start(bf16[64,48,128]{2,1,0:T(8,128)(2,1)S(1)} %collective-permute-done.2.start_hbm) | copy-start | bytes 2359300
  65.1 6.3 %collective-permute-start.3 = (bf16[64,40,128]{2,1,0:T(8,128)(2,1)S(1)}, bf16[64,40,128]{2,1,0:T(8,128)(2,1)S(1)}, u32[]{:S(2)}, u32[]{:S(2)}) collective-permute-start(bf16[64,40,128]{2,1,0:T(8,128)(2,1)S(1)} %all-to-all-done.1.start_ref), channel_id=1, source_target_pairs={{0,1},{1,0},{2,3},{3,2},{4,5},{5,4},{6,7},{7,6},{8,9},{9,8},{10,11... | collective-permute-start | bytes 1966088 | tf_op jit(solution)/shard_map/ppermute | solution.py:655
